TPU v7x, 32 devices: a whole 2x2x4 slice. The times are simulated.
32 devices in a mesh: dp: 32 (over z, y, x, core).
Axes of the slice: x: 2, y: 2, z: 4, core: 2. Of those that a mesh axis runs over, the one named last changes fastest.
Arguments:
- images: bfloat16 [64, 197, 384], P('dp'), may hold values from -6 to 6
- cotangent: bfloat16 [64, 197, 384], P('dp'), may hold values from -6 to 6
- present: int32 [64], P('dp'), may hold values 0 or 1
- params: float32 [2, 1777664], P(None, 'dp'), as said below
- first_moment: float32 [2, 1777664], P(None, 'dp'), as said below
- second_moment: float32 [2, 1777664], P(None, 'dp'), as said below
Outputs:
- outputs: float32 [64, 197, 384], P('dp')
- input_grad: float32 [64, 197, 384], P('dp')
- new_params: float32 [2, 1777664], P(None, 'dp')
- new_first: float32 [2, 1777664], P(None, 'dp')
- new_second: float32 [2, 1777664], P(None, 'dp')
Inputs may be any that keep to these rules, and one draw needn't show every extreme that they name: `params`: gains near 1, weights scaled by their fan-in. `first_moment`: both signs. `second_moment`: every entry positive.
All inputs are finite; a program needn't handle non-finite values. No bound on the sum of `present` on one device may be relied on, other than what follows from the above.
Results may differ from a plain program's by a relative error of at most 0.012.
Values may be sent and summed in bfloat16 or wider, within the bound.
No kernel may reach another device: no remote copies, remote signals or barrier semaphores. Data moves between devices by JAX's collectives and lax.ppermute only.
A program may use at most 128 MiB of HBM per device.

v0:
```python
import functools
import math

import jax
import jax.numpy as jnp
from jax import lax
from jax.experimental import pallas as pl
from jax.experimental.pallas import tpu as pltpu
from jax.sharding import PartitionSpec as P

D = 384
FF = 1536
HEADS = 6
HEAD_DIM = 64
SEQ = 197
MICRO = 2
STEP = 10
P_SIZE = 1774080

LANES = 128
ROWS = 208
TOKENS = MICRO * ROWS
PAIRS = HEADS // 2
BLOCK = 512

eps_norm = 1e-06
beta_one = 0.9
beta_two = 0.999
adam_eps = 1e-08
rate_matrix = 0.1
rate_vector = 0.5
decay_matrix = 0.05
sqrt_half = 0.7071067811865476
inverse_root_tau = 0.3989422804014327

f32 = jnp.float32
bf16 = jnp.bfloat16


def layout():
    return [
        ("ln1_gain", (D,)),
        ("ln1_shift", (D,)),
        ("w_qkv", (D, 3 * D)),
        ("bias_query", (D,)),
        ("bias_value", (D,)),
        ("w_attn_out", (D, D)),
        ("bias_attn_out", (D,)),
        ("ln2_gain", (D,)),
        ("ln2_shift", (D,)),
        ("w_lift", (D, FF)),
        ("bias_lift", (FF,)),
        ("w_drop", (FF, D)),
        ("bias_drop", (D,)),
    ]


def row_offsets():
    offsets, at = {}, 0
    for label, shape in layout():
        offsets[label] = at
        at += math.prod(shape) // LANES
    offsets["end"] = at
    return offsets


ROW = row_offsets()
MLP_ROW = ROW["ln2_gain"]


def matrix_flags(position):
    square = D * D
    lifted = D * FF
    bounds = [
        (2 * D, 2 * D + 3 * square),
        (4 * D + 3 * square, 4 * D + 4 * square),
        (7 * D + 4 * square, 7 * D + 4 * square + lifted),
        (7 * D + 4 * square + lifted + FF, 7 * D + 4 * square + 2 * lifted + FF),
    ]
    flags = jnp.zeros(position.shape, dtype=bool)
    for lower, upper in bounds:
        flags = flags | (position >= lower) & (position < upper)
    return flags


def round_up(value, step):
    return (value + step - 1) // step * step


def dot(a, b, dims):
    return lax.dot_general(a, b, ((dims[0], dims[1]), ((), ())), preferred_element_type=f32)


def dot_nn(a, b):
    return dot(a, b, ((1,), (0,)))


def dot_nt(a, b):
    return dot(a, b, ((1,), (1,)))


def dot_tn(a, b):
    return dot(a, b, ((0,), (0,)))


def read_vector(flat, row, count):
    parts = [flat[row + i : row + i + 1, :] for i in range(count)]
    return jnp.concatenate(parts, axis=1)


def write_vector(flat, row, values):
    for i in range(values.shape[1] // LANES):
        flat[row + i : row + i + 1, :] = values[:, i * LANES : (i + 1) * LANES]


def read_matrix(flat, row, out, depth, width):
    blocks = width // LANES
    for j in range(blocks):
        part = flat[pl.ds(row + j, depth, stride=blocks), :]
        out[:, j * LANES : (j + 1) * LANES] = part.astype(bf16)


def write_matrix(flat, row, values, blocks):
    depth, width = values.shape
    for j in range(width // LANES):
        flat[pl.ds(row + j, depth, stride=blocks), :] = values[:, j * LANES : (j + 1) * LANES]


def normalize(values):
    center = values - jnp.mean(values, -1, keepdims=True)
    rstd = lax.rsqrt(jnp.mean(center * center, -1, keepdims=True) + eps_norm)
    return center * rstd, rstd


def norm_back(incoming, unit, rstd, gain):
    scaled = incoming * gain
    inner = jnp.mean(scaled * unit, -1, keepdims=True)
    back = rstd * (scaled - jnp.mean(scaled, -1, keepdims=True) - unit * inner)
    gain_grad = jnp.sum(incoming * unit, 0, keepdims=True)
    return back, gain_grad, jnp.sum(incoming, 0, keepdims=True)


def head_mask(head):
    lane = lax.broadcasted_iota(jnp.int32, (1, LANES), 1)
    return lane < HEAD_DIM if head == 0 else lane >= HEAD_DIM


def pair_slices(step):
    image, pair = step // PAIRS, step % PAIRS
    rows = pl.ds(pl.multiple_of(image * ROWS, 16), ROWS)
    cols = [pl.ds(pl.multiple_of(t * D + pair * LANES, LANES), LANES) for t in range(3)]
    return rows, cols


def attention_forward(rows_each, first, *refs):
    place, state, low = refs[:3]
    refs = refs[3:]
    if first:
        kept_state, refs = refs[0], refs[1:]
    w_qkv, w_out, gains, normed_one, qkv, probs, mixed, hidden, flat = refs
    padded = low.shape[1]
    for chunk in range(-(-MLP_ROW // rows_each)):
        flat[chunk * rows_each : chunk * rows_each + padded, :] = low[place[chunk]].astype(f32)
    read_matrix(flat, ROW["w_qkv"], w_qkv, D, 3 * D)
    read_matrix(flat, ROW["w_attn_out"], w_out, D, D)
    gain = read_vector(flat, ROW["ln1_gain"], 3)
    shift = read_vector(flat, ROW["ln1_shift"], 3)
    gains[...] = jnp.broadcast_to(gain, gains.shape)
    if first:
        kept_state[...] = jnp.zeros_like(kept_state)
        for image in range(MICRO):
            kept_state[image * ROWS : image * ROWS + SEQ, :] = state[image].astype(f32)
        x = kept_state[...]
    else:
        x = state[...]
    unit, _ = normalize(x)
    normed_one[...] = (unit * gain + shift).astype(bf16)
    bias_query = read_vector(flat, ROW["bias_query"], 3)
    bias = jnp.concatenate(
        [bias_query, jnp.zeros_like(bias_query), read_vector(flat, ROW["bias_value"], 3)], axis=1
    )
    for t in range(3):
        cols = slice(t * D, (t + 1) * D)
        product = dot_nn(normed_one[...], w_qkv[:, cols]) + bias[:, cols]
        qkv[:, cols] = product.astype(bf16)

    def step(at, carry):
        rows, cols = pair_slices(at)
        query, key_rows, value_rows = qkv[rows, cols[0]], qkv[rows, cols[1]], qkv[rows, cols[2]]
        real = lax.broadcasted_iota(jnp.int32, (ROWS, ROWS), 1) < SEQ
        sides = []
        for head in range(2):
            own_key = jnp.where(head_mask(head), key_rows, jnp.zeros_like(key_rows))
            raw = jnp.where(real, dot_nt(query, own_key), -1e30)
            powers = jnp.exp((raw - jnp.max(raw, -1, keepdims=True)) * HEAD_DIM ** (-0.5))
            weight = powers / jnp.sum(powers, -1, keepdims=True)
            probs[at * 2 + head] = weight
            sides.append(dot_nn(weight.astype(bf16), value_rows))
        mixed[rows, pl.ds(pl.multiple_of((at % PAIRS) * LANES, LANES), LANES)] = jnp.where(
            head_mask(0), sides[0], sides[1]
        ).astype(bf16)
        return carry

    lax.fori_loop(0, MICRO * PAIRS, step, 0)
    hidden[...] = x + dot_nn(mixed[...], w_out[...]) + read_vector(flat, ROW["bias_attn_out"], 3)


def mlp_forward(rows_each, last, *refs):
    place_low, place_high, hidden, low, high = refs[:5]
    w_lift, w_drop, gains, normed_two, active, slope, result, flat = refs[5:]
    padded, count = low.shape[1], low.shape[0]
    begin = MLP_ROW // rows_each
    base = begin * rows_each
    for chunk in range(begin, count):
        at = chunk * rows_each - base
        flat[at : at + padded, :] = low[place_low[chunk]].astype(f32)
    for chunk in range(count):
        at = (count + chunk) * rows_each - base
        flat[at : at + padded, :] = high[place_high[chunk]].astype(f32)
    read_matrix(flat, ROW["w_lift"] - base, w_lift, D, FF)
    read_matrix(flat, ROW["w_drop"] - base, w_drop, FF, D)
    gain = read_vector(flat, ROW["ln2_gain"] - base, 3)
    shift = read_vector(flat, ROW["ln2_shift"] - base, 3)
    gains[...] = jnp.broadcast_to(gain, gains.shape)
    bias_lift = read_vector(flat, ROW["bias_lift"] - base, FF // LANES)
    unit, _ = normalize(hidden[...])
    normed_two[...] = (unit * gain + shift).astype(bf16)
    total = hidden[...] + read_vector(flat, ROW["bias_drop"] - base, 3)
    for at in range(0, FF, BLOCK):
        cols = slice(at, at + BLOCK)
        lifted = dot_nn(normed_two[...], w_lift[:, cols]) + bias_lift[:, cols]
        below = 0.5 * (1.0 + lax.erf(lifted * sqrt_half))
        active[:, cols] = (lifted * below).astype(bf16)
        slope[:, cols] = below + lifted * jnp.exp(-0.5 * lifted * lifted) * inverse_root_tau
        total += dot_nn(active[:, cols], w_drop[cols, :])
    if last:
        for image in range(MICRO):
            result[image] = total[image * ROWS : image * ROWS + SEQ, :]
    else:
        result[...] = total


def pack(flat, base, rows_each, first_chunk, place, out):
    padded, count = out.shape[1], out.shape[0]
    for chunk in range(count):
        at = (first_chunk + chunk) * rows_each - base
        out[place[chunk]] = flat[at : at + padded, :].astype(bf16)


def mlp_backward(rows_each, last, *refs):
    if last:
        present, refs = refs[0], refs[1:]
    place_high, incoming, hidden, w_lift, w_drop, gains, normed_two, active, slope = refs[:9]
    refs = refs[9:]
    carry, high, g_hidden, flat = refs[:4]
    count = high.shape[0]
    if last:
        kept = refs[4]
        kept[...] = jnp.zeros_like(kept)
        for image in range(MICRO):
            seed = incoming[image].astype(f32) * present[image].astype(f32)
            kept[image * ROWS : image * ROWS + SEQ, :] = seed
        g = kept[...]
    else:
        g = incoming[...]
    base = MLP_ROW
    end = ROW["end"] - base
    flat[end:, :] = jnp.zeros((flat.shape[0] - end, LANES), f32)
    g_out = g.astype(bf16)
    write_vector(flat, ROW["bias_drop"] - base, jnp.sum(g_out.astype(f32), 0, keepdims=True))
    d_normed = jnp.zeros((TOKENS, D), f32)
    for at in range(0, FF, BLOCK):
        cols = slice(at, at + BLOCK)
        row = ROW["w_drop"] - base + at * (D // LANES)
        write_matrix(flat, row, dot_tn(active[:, cols], g_out), D // LANES)
        d_lifted = (dot_nt(g_out, w_drop[cols, :]) * slope[:, cols]).astype(bf16)
        row = ROW["bias_lift"] - base + at // LANES
        write_vector(flat, row, jnp.sum(d_lifted.astype(f32), 0, keepdims=True))
        row = ROW["w_lift"] - base + at // LANES
        write_matrix(flat, row, dot_tn(normed_two[...], d_lifted), FF // LANES)
        d_normed += dot_nt(d_lifted, w_lift[:, cols])
    unit, rstd = normalize(hidden[...])
    back, gain_grad, shift_grad = norm_back(d_normed, unit, rstd, gains[0:1, :])
    write_vector(flat, ROW["ln2_gain"] - base, gain_grad)
    write_vector(flat, ROW["ln2_shift"] - base, shift_grad)
    g_hidden[...] = g + back
    carry[...] = flat[: carry.shape[0], :]
    pack(flat, base, rows_each, count, place_high, high)


def attention_backward(rows_each, first, *refs):
    place_low, g_hidden, state, w_qkv, w_out, gains, normed_one, qkv, probs, mixed, carry = refs[:11]
    low, input_grad, flat, d_mixed, d_qkv = refs[11:]
    flat[MLP_ROW : MLP_ROW + carry.shape[0], :] = carry[...]
    g_att = g_hidden[...].astype(bf16)
    write_vector(flat, ROW["bias_attn_out"], jnp.sum(g_att.astype(f32), 0, keepdims=True))
    write_matrix(flat, ROW["w_attn_out"], dot_tn(mixed[...], g_att), D // LANES)
    d_mixed[...] = dot_nt(g_att, w_out[...]).astype(bf16)

    def step(at, carried):
        rows, cols = pair_slices(at)
        query, key_rows, value_rows = qkv[rows, cols[0]], qkv[rows, cols[1]], qkv[rows, cols[2]]
        mixed_grad = d_mixed[rows, pl.ds(pl.multiple_of((at % PAIRS) * LANES, LANES), LANES)]
        d_query, d_key, d_value = [], [], []
        for head in range(2):
            own = jnp.where(head_mask(head), mixed_grad, jnp.zeros_like(mixed_grad))
            weight = probs[at * 2 + head]
            d_value.append(dot_tn(weight.astype(bf16), mixed_grad))
            d_probs = dot_nt(own, value_rows)
            inner = jnp.sum(weight * d_probs, -1, keepdims=True)
            d_scores = (weight * (d_probs - inner)).astype(bf16)
            d_query.append(dot_nn(d_scores, key_rows))
            d_key.append(dot_tn(d_scores, query))
        scale = HEAD_DIM ** (-0.5)
        mask = head_mask(0)
        d_qkv[rows, cols[0]] = (jnp.where(mask, d_query[0], d_query[1]) * scale).astype(bf16)
        d_qkv[rows, cols[1]] = (jnp.where(mask, d_key[0], d_key[1]) * scale).astype(bf16)
        d_qkv[rows, cols[2]] = jnp.where(mask, d_value[0], d_value[1]).astype(bf16)
        return carried

    lax.fori_loop(0, MICRO * PAIRS, step, 0)
    query_sum = jnp.sum(d_qkv[:, :D].astype(f32), 0, keepdims=True)
    write_vector(flat, ROW["bias_query"], query_sum)
    value_sum = jnp.sum(d_qkv[:, 2 * D :].astype(f32), 0, keepdims=True)
    write_vector(flat, ROW["bias_value"], value_sum)
    d_normed = jnp.zeros((TOKENS, D), f32)
    for t in range(3):
        cols = slice(t * D, (t + 1) * D)
        part = d_qkv[:, cols]
        row = ROW["w_qkv"] + t * (D // LANES)
        write_matrix(flat, row, dot_tn(normed_one[...], part), 3 * D // LANES)
        d_normed += dot_nt(part, w_qkv[:, cols])
    unit, rstd = normalize(state[...])
    back, gain_grad, shift_grad = norm_back(d_normed, unit, rstd, gains[0:1, :])
    write_vector(flat, ROW["ln1_gain"], gain_grad)
    write_vector(flat, ROW["ln1_shift"], shift_grad)
    total = g_hidden[...] + back
    if first:
        for image in range(MICRO):
            input_grad[image] = total[image * ROWS : image * ROWS + SEQ, :]
    else:
        input_grad[...] = total
    pack(flat, 0, rows_each, 0, place_low, low)


def call(body, name, inputs, outputs, scratch, scalars=0, flops=0):
    in_specs = [pl.BlockSpec(memory_space=pltpu.SMEM)] * scalars
    in_specs += [pl.BlockSpec(memory_space=pltpu.VMEM)] * (len(inputs) - scalars)
    shapes = [jax.ShapeDtypeStruct(shape, dtype) for shape, dtype in outputs]
    moved = sum(math.prod(s.shape) * s.dtype.itemsize for s in list(inputs) + shapes)
    return pl.pallas_call(
        body,
        name=name,
        out_shape=shapes,
        in_specs=in_specs,
        out_specs=[pl.BlockSpec(memory_space=pltpu.VMEM)] * len(shapes),
        scratch_shapes=scratch,
        compiler_params=pltpu.CompilerParams(vmem_limit_bytes=40 * 1024 * 1024),
        cost_estimate=pl.CostEstimate(flops=flops, bytes_accessed=moved, transcendentals=0),
    )(*inputs)


def xor_permute(values, bit, size):
    return lax.ppermute(values, "dp", [(i, i ^ (1 << bit)) for i in range(size)])


def half_orders(bits):
    top = list(range(bits - 2, 2, -1))
    return (top + [1, 2, 0], top + [2, 1, 0])


def places(me, size, order):
    relative = (me ^ jnp.arange(size // 2, dtype=jnp.int32)) & (size // 2 - 1)
    place = jnp.zeros_like(relative)
    for digit, bit in enumerate(order):
        place = place | (((relative >> bit) & 1) << digit)
    return place


def gather(shard, me, size, bits):
    top = (me >> (bits - 1)) & 1
    other = xor_permute(shard, bits - 1, size)
    halves = [jnp.where(top == 0, shard, other)[None], jnp.where(top == 0, other, shard)[None]]
    orders = half_orders(bits)
    for step in range(bits - 1):
        moved = [xor_permute(halves[h], orders[h][step], size) for h in range(2)]
        halves = [jnp.concatenate([halves[h], moved[h]]) for h in range(2)]
    return halves


def scatter_half(half, order, size):
    for bit in reversed(order):
        middle = half.shape[0] // 2
        received = xor_permute(half[middle:], bit, size)
        half = (half[:middle].astype(f32) + received.astype(f32)).astype(bf16)
    return half[0]


def scatter_top(low, high, me, size, bits):
    top = (me >> (bits - 1)) & 1
    sent = jnp.where(top == 0, high, low)
    kept = jnp.where(top == 0, low, high)
    received = xor_permute(sent, bits - 1, size)
    return kept.astype(f32) + received.astype(f32)


def shards(size, images, cotangent, present, params, first_moment, second_moment):
    bits = size.bit_length() - 1
    width = params.shape[1]
    rows_each = width // LANES
    padded = round_up(rows_each, 16)
    half = size // 2
    me = lax.axis_index("dp")
    orders = half_orders(bits)
    place = [places(me, size, order) for order in orders]

    compact = params.astype(bf16).reshape(2, rows_each, LANES)
    compact = jnp.pad(compact, ((0, 0), (0, padded - rows_each), (0, 0)))
    low, high = [None, None], [None, None]
    for layer in range(2):
        low[layer], high[layer] = gather(compact[layer], me, size, bits)

    low_flat = pltpu.VMEM((-(-MLP_ROW // rows_each) * rows_each + padded, LANES), f32)
    begin = MLP_ROW // rows_each
    high_flat = pltpu.VMEM(((size - begin) * rows_each + padded, LANES), f32)
    square = TOKENS * D * D
    core_flops = 2 * 2 * MICRO * HEADS * ROWS * ROWS * HEAD_DIM

    state = images
    saved = []
    for layer in range(2):
        first = layer == 0
        outputs = [((TOKENS, D), f32)] if first else []
        outputs += [
            ((D, 3 * D), bf16),
            ((D, D), bf16),
            ((8, D), f32),
            ((TOKENS, D), bf16),
            ((TOKENS, 3 * D), bf16),
            ((MICRO * HEADS, ROWS, ROWS), f32),
            ((TOKENS, D), bf16),
            ((TOKENS, D), f32),
        ]
        made = call(
            functools.partial(attention_forward, rows_each, first),
            "attention_forward",
            [place[0], state, low[layer]],
            outputs,
            [low_flat],
            scalars=1,
            flops=8 * square + core_flops,
        )
        if first:
            state, made = made[0], made[1:]
        w_qkv, w_out, gains_one, normed_one, qkv, probs, mixed, hidden = made
        last = layer == 1
        w_lift, w_drop, gains_two, normed_two, active, slope, result = call(
            functools.partial(mlp_forward, rows_each, last),
            "mlp_forward",
            [place[0], place[1], hidden, low[layer], high[layer]],
            [
                ((D, FF), bf16),
                ((FF, D), bf16),
                ((8, D), f32),
                ((TOKENS, D), bf16),
                ((TOKENS, FF), bf16),
                ((TOKENS, FF), f32),
                ((MICRO, SEQ, D) if last else (TOKENS, D), f32),
            ],
            [high_flat],
            scalars=2,
            flops=16 * square,
        )
        one = (state, w_qkv, w_out, gains_one, normed_one, qkv, probs, mixed)
        two = (hidden, w_lift, w_drop, gains_two, normed_two, active, slope)
        saved.append((one, two))
        state = result
    outputs = state

    carry_rows = round_up(half * rows_each - MLP_ROW + padded - rows_each, 8)
    incoming = cotangent
    owned = [None, None]
    for layer in (1, 0):
        first, last = layer == 0, layer == 1
        one, two = saved[layer]
        scratch = [pltpu.VMEM((size * rows_each + padded - MLP_ROW, LANES), f32)]
        if last:
            scratch.append(pltpu.VMEM((TOKENS, D), f32))
        inputs = [present] if last else []
        carry, high_grads, g_hidden = call(
            functools.partial(mlp_backward, rows_each, last),
            "mlp_backward",
            inputs + [place[1], incoming, *two],
            [((carry_rows, LANES), f32), ((half, padded, LANES), bf16), ((TOKENS, D), f32)],
            scratch,
            scalars=2 if last else 1,
            flops=32 * square,
        )
        low_grads, incoming = call(
            functools.partial(attention_backward, rows_each, first),
            "attention_backward",
            [place[0], g_hidden, *one, carry],
            [
                ((half, padded, LANES), bf16),
                ((MICRO, SEQ, D) if first else (TOKENS, D), f32),
            ],
            [
                pltpu.VMEM((MLP_ROW + carry_rows, LANES), f32),
                pltpu.VMEM((TOKENS, D), bf16),
                pltpu.VMEM((TOKENS, 3 * D), bf16),
            ],
            scalars=1,
            flops=16 * square + 2 * core_flops,
        )
        owned_high = scatter_half(high_grads, orders[1], size)
        owned_low = scatter_half(low_grads, orders[0], size)
        total = scatter_top(owned_low, owned_high, me, size, bits)
        owned[layer] = total[:rows_each].reshape(width)

    grads = jnp.stack(owned)
    position = me * width + jnp.arange(width, dtype=jnp.int32)
    flags = matrix_flags(position)[None, :]
    rate = jnp.where(flags, rate_matrix, rate_vector)
    decay = jnp.where(flags, decay_matrix, 0.0)
    new_first = beta_one * first_moment + (1.0 - beta_one) * grads
    new_second = beta_two * second_moment + (1.0 - beta_two) * grads * grads
    first_hat = new_first / (1.0 - beta_one**STEP)
    second_hat = new_second / (1.0 - beta_two**STEP)
    new_params = params - rate * (first_hat / (jnp.sqrt(second_hat) + adam_eps) + decay * params)
    return (outputs, incoming, new_params, new_first, new_second)


def solution(mesh):
    in_specs = (
        P("dp", None, None),
        P("dp", None, None),
        P("dp"),
        P(None, "dp"),
        P(None, "dp"),
        P(None, "dp"),
    )
    out_specs = (
        P("dp", None, None),
        P("dp", None, None),
        P(None, "dp"),
        P(None, "dp"),
        P(None, "dp"),
    )
    body = functools.partial(shards, mesh.shape["dp"])
    return jax.shard_map(body, mesh=mesh, in_specs=in_specs, out_specs=out_specs, check_vma=False)
```

profile of v0, /device:TPU:0, one launch (start us, length us, event | category | flops | bytes accessed | tf_op | source)
XLA Modules:
  0.0 182.7 jit_solution(14330780560593763052)
XLA Ops:
  2.3 4.1 %collective-permute-start.9 = (bf16[448,128]{1,0:T(8,128)(2,1)S(1)}, bf16[448,128]{1,0:T(8,128)(2,1)S(1)}, u32[]{:S(2)}, u32[]{:S(2)}) collective-permute-start(bf16[448,128]{1,0:T(8,128)(2,1)S(1)} %get-tuple-element.120), channel_id=1, source_target_pairs={{0,16},{1,17},{2,18},{3,19},{4,20},{5,21},{6,22},{7,23},{8,24},{9,... | collective-permute-start | bytes 344072 | tf_op jit(solution)/shard_map/ppermute | solution.py:364
  6.5 8.8 %collective-permute-done.9 = bf16[448,128]{1,0:T(8,128)(2,1)S(1)} collective-permute-done((bf16[448,128]{1,0:T(8,128)(2,1)S(1)}, bf16[448,128]{1,0:T(8,128)(2,1)S(1)}, u32[]{:S(2)}, u32[]{:S(2)}) %collective-permute-start.9) | collective-permute-done | bytes 114720 | tf_op jit(solution)/shard_map/ppermute | solution.py:364
  15.3 1.6 collective-permute-done
  22.0 1.8 collective-permute-done.1
  30.0 1.6 collective-permute-start.15
  37.1 1.7 collective-permute-done.15
  40.4 8.2 %collective-permute-done.3 = bf16[4,448,128]{2,1,0:T(8,128)(2,1)S(1)} collective-permute-done((bf16[4,448,128]{2,1,0:T(8,128)(2,1)S(1)}, bf16[4,448,128]{2,1,0:T(8,128)(2,1)S(1)}, u32[]{:S(2)}, u32[]{:S(2)}) %collective-permute-start.3) | collective-permute-done | bytes 458784 | tf_op jit(solution)/shard_map/ppermute | solution.py:364
  49.5 7.5 %collective-permute-done.12 = bf16[4,448,128]{2,1,0:T(8,128)(2,1)S(1)} collective-permute-done((bf16[4,448,128]{2,1,0:T(8,128)(2,1)S(1)}, bf16[4,448,128]{2,1,0:T(8,128)(2,1)S(1)}, u32[]{:S(2)}, u32[]{:S(2)}) %collective-permute-start.12) | collective-permute-done | bytes 458784 | tf_op jit(solution)/shard_map/ppermute | solution.py:364
  58.2 7.8 %attention_forward.2 = (f32[416,384]{1,0:T(8,128)S(1)}, bf16[384,1152]{1,0:T(8,128)(2,1)S(1)}, bf16[384,384]{1,0:T(8,128)(2,1)S(1)}, f32[8,384]{1,0:T(8,128)S(1)...) custom-call(s32[16]{0:T(128)S(1)} %get-tuple-element.123.refs_0_, ...), custom_call_target="tpu_custom_call" | custom-call | flops 623640576 | bytes 8281664 | tf_op jit(solution)/shard_map/attention_forward/pallas_call | solution.py:351
  68.5 3.8 %mlp_forward.2 = (bf16[384,1536]{1,0:T(8,128)(2,1)S(1)}, bf16[1536,384]{1,0:T(8,128)(2,1)S(1)}, f32[8,384]{1,0:T(8,128)S(1)}, bf16[416,384]{1,0:T(8,128)(2,1)S(1...) custom-call(s32[16]{0:T(128)S(1)} %get-tuple-element.123.refs_0_, ...), custom_call_target="tpu_custom_call" | custom-call | flops 981467136 | bytes 11473024 | tf_op jit(solution)/shard_map/mlp_forward/pallas_call | solution.py:351
  73.2 7.6 %attention_forward.3 = (bf16[384,1152]{1,0:T(8,128)(2,1)S(1)}, bf16[384,384]{1,0:T(8,128)(2,1)S(1)}, f32[8,384]{1,0:T(8,128)S(1)}, bf16[416,384]{1,0:T(8,128)(2,...) custom-call(s32[16]{0:T(128)S(1)} %get-tuple-element.123.refs_0_, ...), custom_call_target="tpu_custom_call" | custom-call | flops 623640576 | bytes 7979072 | tf_op jit(solution)/shard_map/attention_forward/pallas_call | solution.py:351
  86.3 3.8 %mlp_forward.3 = (bf16[384,1536]{1,0:T(8,128)(2,1)S(1)}, bf16[1536,384]{1,0:T(8,128)(2,1)S(1)}, f32[8,384]{1,0:T(8,128)S(1)}, bf16[416,384]{1,0:T(8,128)(2,1)S(1...) custom-call(s32[16]{0:T(128)S(1)} %get-tuple-element.123.refs_0_, ...), custom_call_target="tpu_custom_call" | custom-call | flops 981467136 | bytes 11439232 | tf_op jit(solution)/shard_map/mlp_forward/pallas_call | solution.py:351
  92.4 1.7 copy-done.1
  94.1 4.4 %mlp_backward.2 = (f32[2336,128]{1,0:T(8,128)S(1)}, bf16[16,448,128]{2,1,0:T(8,128)(2,1)S(1)}, f32[416,384]{1,0:T(8,128)S(1)}) custom-call(s32[2]{0:T(128)S(1)} %copy-done.37, s32[16]{0:T(128)S(1)} %get-tuple-element.122.refs_1_.refs_0_, bf16[2,197,384]{2,1,0:T(8,128)(2,1)S(1)} %copy.16.refs_2_, f32[416,384]{1,0:T(8,128)S(1)} %get-tuple-element.48.refs_2_.refs_3_, ...), custom_call_target="tpu_custom_call" | custom-call | flops 1962934272 | bytes 11136584 | tf_op jit(solution)/shard_map/mlp_backward/pallas_call | solution.py:351
  101.4 8.8 %attention_backward.2 = (bf16[16,448,128]{2,1,0:T(8,128)(2,1)S(1)}, f32[416,384]{1,0:T(8,128)S(1)}) custom-call(s32[16]{0:T(128)S(1)} %get-tuple-element.123.refs_0_, f32[416,384]{1,0:T(8,128)S(1)} %get-tuple-element.56.refs_1_, f32[416,384]{1,0:T(8,128)S(1)} %get-tuple-element.47.refs_1_.refs_2_, bf16[384,1152]{1,0:T(8,128)(2,1)S(1)} %copy-done.18, ...), custom_call_target="tpu_custom_call" | custom-call | flops 1247281152 | bytes 9814080 | tf_op jit(solution)/shard_map/attention_backward/pallas_call | solution.py:351
  111.9 4.4 %mlp_backward.3 = (f32[2336,128]{1,0:T(8,128)S(1)}, bf16[16,448,128]{2,1,0:T(8,128)(2,1)S(1)}, f32[416,384]{1,0:T(8,128)S(1)}) custom-call(s32[16]{0:T(128)S(1)} %get-tuple-element.122.refs_1_.refs_0_, f32[416,384]{1,0:T(8,128)S(1)} %get-tuple-element.65.refs_1_, f32[416,384]{1,0:T(8,128)S(1)} %get-tuple-element.46.refs_2_, bf16[384,1536]{1,0:T(8,128)(2,1)S(1)} %copy-done.8, ...), custom_call_target="tpu_custom_call" | custom-call | flops 1962934272 | bytes 11472960 | tf_op jit(solution)/shard_map/mlp_backward/pallas_call | solution.py:351
  116.4 8.8 %attention_backward.3 = (bf16[16,448,128]{2,1,0:T(8,128)(2,1)S(1)}, f32[2,197,384]{2,1,0:T(8,128)S(1)}) custom-call(s32[16]{0:T(128)S(1)} %get-tuple-element.123.refs_0_, f32[416,384]{1,0:T(8,128)S(1)} %get-tuple-element.72.refs_1_, f32[416,384]{1,0:T(8,128)S(1)} %copy-done.20, bf16[384,1152]{1,0:T(8,128)(2,1)S(1)} %copy-done.16, ...), custom_call_target="tpu_custom_call" | custom-call | flops 1247281152 | bytes 9780288 | tf_op jit(solution)/shard_map/attention_backward/pallas_call | solution.py:351
  134.1 8.3 %collective-permute-done.28 = bf16[4,448,128]{2,1,0:T(8,128)(2,1)S(1)} collective-permute-done((bf16[4,448,128]{2,1,0:T(8,128)(2,1)S(1)}, bf16[4,448,128]{2,1,0:T(8,128)(2,1)S(1)}, u32[]{:S(2)}, u32[]{:S(2)}) %collective-permute-start.28) | collective-permute-done | bytes 458784 | tf_op jit(solution)/shard_map/ppermute | solution.py:364
  145.7 6.4 %collective-permute-done.19 = bf16[4,448,128]{2,1,0:T(8,128)(2,1)S(1)} collective-permute-done((bf16[4,448,128]{2,1,0:T(8,128)(2,1)S(1)}, bf16[4,448,128]{2,1,0:T(8,128)(2,1)S(1)}, u32[]{:S(2)}, u32[]{:S(2)}) %collective-permute-start.19) | collective-permute-done | bytes 458784 | tf_op jit(solution)/shard_map/ppermute | solution.py:364
  155.6 3.4 %collective-permute-done.29 = bf16[2,448,128]{2,1,0:T(8,128)(2,1)S(1)} collective-permute-done((bf16[2,448,128]{2,1,0:T(8,128)(2,1)S(1)}, bf16[2,448,128]{2,1,0:T(8,128)(2,1)S(1)}, u32[]{:S(2)}, u32[]{:S(2)}) %collective-permute-start.29) | collective-permute-done | bytes 229408 | tf_op jit(solution)/shard_map/ppermute | solution.py:364
  166.0 3.6 %collective-permute-start.35 = (bf16[448,128]{1,0:T(8,128)(2,1)S(1)}, bf16[448,128]{1,0:T(8,128)(2,1)S(1)}, u32[]{:S(2)}, u32[]{:S(2)}) collective-permute-start(bf16[448,128]{1,0:T(8,128)(2,1)S(1)} %get-tuple-element.110), channel_id=1, source_target_pairs={{0,16},{1,17},{2,18},{3,19},{4,20},{5,21},{6,22},{7,23},{8,24},{9,... | collective-permute-start | bytes 344072 | tf_op jit(solution)/shard_map/ppermute | solution.py:364
  171.5 2.7 %collective-permute-start.26 = (bf16[448,128]{1,0:T(8,128)(2,1)S(1)}, bf16[448,128]{1,0:T(8,128)(2,1)S(1)}, u32[]{:S(2)}, u32[]{:S(2)}) collective-permute-start(bf16[448,128]{1,0:T(8,128)(2,1)S(1)} %get-tuple-element.108), channel_id=1, source_target_pairs={{0,16},{1,17},{2,18},{3,19},{4,20},{5,21},{6,22},{7,23},{8,24},{9,... | collective-permute-start | bytes 344072 | tf_op jit(solution)/shard_map/ppermute | solution.py:364
  174.4 5.2 %collective-permute-done.26 = bf16[448,128]{1,0:T(8,128)(2,1)S(1)} collective-permute-done((bf16[448,128]{1,0:T(8,128)(2,1)S(1)}, bf16[448,128]{1,0:T(8,128)(2,1)S(1)}, u32[]{:S(2)}, u32[]{:S(2)}) %collective-permute-start.26) | collective-permute-done | bytes 114720 | tf_op jit(solution)/shard_map/ppermute | solution.py:364
  179.9 2.8 %multiply_subtract_fusion = (f32[2,55552]{1,0:T(2,128)}, f32[2,55552]{1,0:T(2,128)}, f32[2,55552]{1,0:T(2,128)}) fusion(f32[2,55552]{1,0:T(2,128)S(1)} %copy-done.44, f32[55552]{0:T(1024)S(1)} %get-tuple-element.124, f32[55552]{0:T(1024)S(1)} %get-tuple-element.125, f32[1,55552]{1,0:T(1,128)S(1)} %bitcast.50, f32[1,55552]{1,0:T(1,128)S(1)} %bitcast.51, ...), kind=kLoop, calls=%fused_computation.23 | loop fusion | flops 1777664 | bytes 3555328 | tf_op jit(solution)/shard_map/sub | solution.py:529
  (227 shorter events, 62.6 us)
Async XLA Ops:
  2.3 13.0 %collective-permute-start.9 = (bf16[448,128]{1,0:T(8,128)(2,1)S(1)}, bf16[448,128]{1,0:T(8,128)(2,1)S(1)}, u32[]{:S(2)}, u32[]{:S(2)}) collective-permute-start(bf16[448,128]{1,0:T(8,128)(2,1)S(1)} %get-tuple-element.120), channel_id=1, source_target_pairs={{0,16},{1,17},{2,18},{3,19},{4,20},{5,21},{6,22},{7,23},{8,24},{9,... | collective-permute-start | bytes 344072 | tf_op jit(solution)/shard_map/ppermute | solution.py:364
  6.4 10.5 %collective-permute-start = (bf16[448,128]{1,0:T(8,128)(2,1)S(1)}, bf16[448,128]{1,0:T(8,128)(2,1)S(1)}, u32[]{:S(2)}, u32[]{:S(2)}) collective-permute-start(bf16[448,128]{1,0:T(8,128)(2,1)S(1)} %get-tuple-element.121), channel_id=1, source_target_pairs={{0,16},{1,17},{2,18},{3,19},{4,20},{5,21},{6,22},{7,23},{8,24},{9,... | collective-permute-start | bytes 344072 | tf_op jit(solution)/shard_map/ppermute | solution.py:364
  20.0 8.4 %collective-permute-start.10 = (bf16[1,448,128]{2,1,0:T(8,128)(2,1)S(1)}, bf16[1,448,128]{2,1,0:T(8,128)(2,1)S(1)}, u32[]{:S(2)}, u32[]{:S(2)}) collective-permute-start(bf16[1,448,128]{2,1,0:T(8,128)(2,1)S(1)} %get-tuple-element.113), channel_id=1, source_target_pairs={{0,8},{1,9},{2,10},{3,11},{4,12},{5,13},{6,14},{7,15},{8,0},{9,1},... | collective-permute-start | bytes 344072 | tf_op jit(solution)/shard_map/ppermute | solution.py:364
  20.7 9.3 %collective-permute-start.14 = (bf16[1,448,128]{2,1,0:T(8,128)(2,1)S(1)}, bf16[1,448,128]{2,1,0:T(8,128)(2,1)S(1)}, u32[]{:S(2)}, u32[]{:S(2)}) collective-permute-start(bf16[1,448,128]{2,1,0:T(8,128)(2,1)S(1)} %get-tuple-element.101), channel_id=1, source_target_pairs={{0,8},{1,9},{2,10},{3,11},{4,12},{5,13},{6,14},{7,15},{8,0},{9,1},... | collective-permute-start | bytes 344072 | tf_op jit(solution)/shard_map/ppermute | solution.py:364
  23.8 9.2 %collective-permute-start.2 = (bf16[2,448,128]{2,1,0:T(8,128)(2,1)S(1)}, bf16[2,448,128]{2,1,0:T(8,128)(2,1)S(1)}, u32[]{:S(2)}, u32[]{:S(2)}) collective-permute-start(bf16[2,448,128]{2,1,0:T(8,128)(2,1)S(1)} %pad_maximum_fusion.9), channel_id=1, source_target_pairs={{0,2},{1,3},{2,0},{3,1},{4,6},{5,7},{6,4},{7,5},{8,10},{9,11},{10,... | collective-permute-start | bytes 688136 | tf_op jit(solution)/shard_map/ppermute | solution.py:364
  30.0 8.7 %collective-permute-start.15 = (bf16[2,448,128]{2,1,0:T(8,128)(2,1)S(1)}, bf16[2,448,128]{2,1,0:T(8,128)(2,1)S(1)}, u32[]{:S(2)}, u32[]{:S(2)}) collective-permute-start(bf16[2,448,128]{2,1,0:T(8,128)(2,1)S(1)} %pad_maximum_fusion.12), channel_id=1, source_target_pairs={{0,4},{1,5},{2,6},{3,7},{4,0},{5,1},{6,2},{7,3},{8,12},{9,13},{10,... | collective-permute-start | bytes 688136 | tf_op jit(solution)/shard_map/ppermute | solution.py:364
  33.1 15.5 %collective-permute-start.3 = (bf16[4,448,128]{2,1,0:T(8,128)(2,1)S(1)}, bf16[4,448,128]{2,1,0:T(8,128)(2,1)S(1)}, u32[]{:S(2)}, u32[]{:S(2)}) collective-permute-start(bf16[4,448,128]{2,1,0:T(8,128)(2,1)S(1)} %pad_maximum_fusion.4), channel_id=1, source_target_pairs={{0,4},{1,5},{2,6},{3,7},{4,0},{5,1},{6,2},{7,3},{8,12},{9,13},{10,... | collective-permute-start | bytes 1376264 | tf_op jit(solution)/shard_map/ppermute | solution.py:364
  33.9 14.9 %collective-permute-start.7 = (bf16[4,448,128]{2,1,0:T(8,128)(2,1)S(1)}, bf16[4,448,128]{2,1,0:T(8,128)(2,1)S(1)}, u32[]{:S(2)}, u32[]{:S(2)}) collective-permute-start(bf16[4,448,128]{2,1,0:T(8,128)(2,1)S(1)} %pad_maximum_fusion.5), channel_id=1, source_target_pairs={{0,2},{1,3},{2,0},{3,1},{4,6},{5,7},{6,4},{7,5},{8,10},{9,11},{10,... | collective-permute-start | bytes 1376264 | tf_op jit(solution)/shard_map/ppermute | solution.py:364
  35.6 21.3 %collective-permute-start.12 = (bf16[4,448,128]{2,1,0:T(8,128)(2,1)S(1)}, bf16[4,448,128]{2,1,0:T(8,128)(2,1)S(1)}, u32[]{:S(2)}, u32[]{:S(2)}) collective-permute-start(bf16[4,448,128]{2,1,0:T(8,128)(2,1)S(1)} %pad_maximum_fusion.6), channel_id=1, source_target_pairs={{0,4},{1,5},{2,6},{3,7},{4,0},{5,1},{6,2},{7,3},{8,12},{9,13},{10,... | collective-permute-start | bytes 1376264 | tf_op jit(solution)/shard_map/ppermute | solution.py:364
  38.8 18.3 %collective-permute-start.16 = (bf16[4,448,128]{2,1,0:T(8,128)(2,1)S(1)}, bf16[4,448,128]{2,1,0:T(8,128)(2,1)S(1)}, u32[]{:S(2)}, u32[]{:S(2)}) collective-permute-start(bf16[4,448,128]{2,1,0:T(8,128)(2,1)S(1)} %pad_maximum_fusion.7), channel_id=1, source_target_pairs={{0,2},{1,3},{2,0},{3,1},{4,6},{5,7},{6,4},{7,5},{8,10},{9,11},{10,... | collective-permute-start | bytes 1376264 | tf_op jit(solution)/shard_map/ppermute | solution.py:364
  48.7 9.4 %collective-permute-start.4 = (bf16[8,448,128]{2,1,0:T(8,128)(2,1)S(1)}, bf16[8,448,128]{2,1,0:T(8,128)(2,1)S(1)}, u32[]{:S(2)}, u32[]{:S(2)}) collective-permute-start(bf16[8,448,128]{2,1,0:T(8,128)(2,1)S(1)} %pad_maximum_fusion), channel_id=1, source_target_pairs={{0,1},{1,0},{2,3},{3,2},{4,5},{5,4},{6,7},{7,6},{8,9},{9,8},{10,11... | collective-permute-start | bytes 2752520 | tf_op jit(solution)/shard_map/ppermute | solution.py:364
  48.9 18.6 %collective-permute-start.8 = (bf16[8,448,128]{2,1,0:T(8,128)(2,1)S(1)}, bf16[8,448,128]{2,1,0:T(8,128)(2,1)S(1)}, u32[]{:S(2)}, u32[]{:S(2)}) collective-permute-start(bf16[8,448,128]{2,1,0:T(8,128)(2,1)S(1)} %pad_maximum_fusion.1), channel_id=1, source_target_pairs={{0,1},{1,0},{2,3},{3,2},{4,5},{5,4},{6,7},{7,6},{8,9},{9,8},{10,11... | collective-permute-start | bytes 2752520 | tf_op jit(solution)/shard_map/ppermute | solution.py:364
  57.0 16.0 %collective-permute-start.13 = (bf16[8,448,128]{2,1,0:T(8,128)(2,1)S(1)}, bf16[8,448,128]{2,1,0:T(8,128)(2,1)S(1)}, u32[]{:S(2)}, u32[]{:S(2)}) collective-permute-start(bf16[8,448,128]{2,1,0:T(8,128)(2,1)S(1)} %pad_maximum_fusion.2), channel_id=1, source_target_pairs={{0,1},{1,0},{2,3},{3,2},{4,5},{5,4},{6,7},{7,6},{8,9},{9,8},{10,11... | collective-permute-start | bytes 2752520 | tf_op jit(solution)/shard_map/ppermute | solution.py:364
  57.2 25.2 %collective-permute-start.17 = (bf16[8,448,128]{2,1,0:T(8,128)(2,1)S(1)}, bf16[8,448,128]{2,1,0:T(8,128)(2,1)S(1)}, u32[]{:S(2)}, u32[]{:S(2)}) collective-permute-start(bf16[8,448,128]{2,1,0:T(8,128)(2,1)S(1)} %pad_maximum_fusion.3), channel_id=1, source_target_pairs={{0,1},{1,0},{2,3},{3,2},{4,5},{5,4},{6,7},{7,6},{8,9},{9,8},{10,11... | collective-permute-start | bytes 2752520 | tf_op jit(solution)/shard_map/ppermute | solution.py:364
  110.3 18.3 %collective-permute-start.27 = (bf16[8,448,128]{2,1,0:T(8,128)(2,1)S(1)}, bf16[8,448,128]{2,1,0:T(8,128)(2,1)S(1)}, u32[]{:S(2)}, u32[]{:S(2)}) collective-permute-start(bf16[8,448,128]{2,1,0:T(8,128)(2,1)S(1)} %slice.128), channel_id=1, source_target_pairs={{0,1},{1,0},{2,3},{3,2},{4,5},{5,4},{6,7},{7,6},{8,9},{9,8},{10,11... | collective-permute-start | bytes 2752520 | tf_op jit(solution)/shard_map/ppermute | solution.py:364
  110.5 19.9 %collective-permute-start.31 = (bf16[8,448,128]{2,1,0:T(8,128)(2,1)S(1)}, bf16[8,448,128]{2,1,0:T(8,128)(2,1)S(1)}, u32[]{:S(2)}, u32[]{:S(2)}) collective-permute-start(bf16[8,448,128]{2,1,0:T(8,128)(2,1)S(1)} %slice.136), channel_id=1, source_target_pairs={{0,1},{1,0},{2,3},{3,2},{4,5},{5,4},{6,7},{7,6},{8,9},{9,8},{10,11... | collective-permute-start | bytes 2752520 | tf_op jit(solution)/shard_map/ppermute | solution.py:364
  128.9 13.4 %collective-permute-start.28 = (bf16[4,448,128]{2,1,0:T(8,128)(2,1)S(1)}, bf16[4,448,128]{2,1,0:T(8,128)(2,1)S(1)}, u32[]{:S(2)}, u32[]{:S(2)}) collective-permute-start(bf16[4,448,128]{2,1,0:T(8,128)(2,1)S(1)} %slice.159), channel_id=1, source_target_pairs={{0,4},{1,5},{2,6},{3,7},{4,0},{5,1},{6,2},{7,3},{8,12},{9,13},{10,... | collective-permute-start | bytes 1376264 | tf_op jit(solution)/shard_map/ppermute | solution.py:364
  130.7 13.5 %collective-permute-start.32 = (bf16[4,448,128]{2,1,0:T(8,128)(2,1)S(1)}, bf16[4,448,128]{2,1,0:T(8,128)(2,1)S(1)}, u32[]{:S(2)}, u32[]{:S(2)}) collective-permute-start(bf16[4,448,128]{2,1,0:T(8,128)(2,1)S(1)} %slice.165), channel_id=1, source_target_pairs={{0,2},{1,3},{2,0},{3,1},{4,6},{5,7},{6,4},{7,5},{8,10},{9,11},{10,... | collective-permute-start | bytes 1376264 | tf_op jit(solution)/shard_map/ppermute | solution.py:364
  132.6 19.6 %collective-permute-start.19 = (bf16[4,448,128]{2,1,0:T(8,128)(2,1)S(1)}, bf16[4,448,128]{2,1,0:T(8,128)(2,1)S(1)}, u32[]{:S(2)}, u32[]{:S(2)}) collective-permute-start(bf16[4,448,128]{2,1,0:T(8,128)(2,1)S(1)} %slice.145), channel_id=1, source_target_pairs={{0,4},{1,5},{2,6},{3,7},{4,0},{5,1},{6,2},{7,3},{8,12},{9,13},{10,... | collective-permute-start | bytes 1376264 | tf_op jit(solution)/shard_map/ppermute | solution.py:364
  133.4 20.6 %collective-permute-start.23 = (bf16[4,448,128]{2,1,0:T(8,128)(2,1)S(1)}, bf16[4,448,128]{2,1,0:T(8,128)(2,1)S(1)}, u32[]{:S(2)}, u32[]{:S(2)}) collective-permute-start(bf16[4,448,128]{2,1,0:T(8,128)(2,1)S(1)} %slice.151), channel_id=1, source_target_pairs={{0,2},{1,3},{2,0},{3,1},{4,6},{5,7},{6,4},{7,5},{8,10},{9,11},{10,... | collective-permute-start | bytes 1376264 | tf_op jit(solution)/shard_map/ppermute | solution.py:364
  142.5 16.5 %collective-permute-start.29 = (bf16[2,448,128]{2,1,0:T(8,128)(2,1)S(1)}, bf16[2,448,128]{2,1,0:T(8,128)(2,1)S(1)}, u32[]{:S(2)}, u32[]{:S(2)}) collective-permute-start(bf16[2,448,128]{2,1,0:T(8,128)(2,1)S(1)} %slice.161), channel_id=1, source_target_pairs={{0,2},{1,3},{2,0},{3,1},{4,6},{5,7},{6,4},{7,5},{8,10},{9,11},{10,... | collective-permute-start | bytes 688136 | tf_op jit(solution)/shard_map/ppermute | solution.py:364
  144.3 15.5 %collective-permute-start.33 = (bf16[2,448,128]{2,1,0:T(8,128)(2,1)S(1)}, bf16[2,448,128]{2,1,0:T(8,128)(2,1)S(1)}, u32[]{:S(2)}, u32[]{:S(2)}) collective-permute-start(bf16[2,448,128]{2,1,0:T(8,128)(2,1)S(1)} %slice.167), channel_id=1, source_target_pairs={{0,4},{1,5},{2,6},{3,7},{4,0},{5,1},{6,2},{7,3},{8,12},{9,13},{10,... | collective-permute-start | bytes 688136 | tf_op jit(solution)/shard_map/ppermute | solution.py:364
  152.3 10.3 %collective-permute-start.20 = (bf16[2,448,128]{2,1,0:T(8,128)(2,1)S(1)}, bf16[2,448,128]{2,1,0:T(8,128)(2,1)S(1)}, u32[]{:S(2)}, u32[]{:S(2)}) collective-permute-start(bf16[2,448,128]{2,1,0:T(8,128)(2,1)S(1)} %slice.147), channel_id=1, source_target_pairs={{0,2},{1,3},{2,0},{3,1},{4,6},{5,7},{6,4},{7,5},{8,10},{9,11},{10,... | collective-permute-start | bytes 688136 | tf_op jit(solution)/shard_map/ppermute | solution.py:364
  154.2 9.3 %collective-permute-start.24 = (bf16[2,448,128]{2,1,0:T(8,128)(2,1)S(1)}, bf16[2,448,128]{2,1,0:T(8,128)(2,1)S(1)}, u32[]{:S(2)}, u32[]{:S(2)}) collective-permute-start(bf16[2,448,128]{2,1,0:T(8,128)(2,1)S(1)} %slice.153), channel_id=1, source_target_pairs={{0,4},{1,5},{2,6},{3,7},{4,0},{5,1},{6,2},{7,3},{8,12},{9,13},{10,... | collective-permute-start | bytes 688136 | tf_op jit(solution)/shard_map/ppermute | solution.py:364
  (61 other events, 338.0 us)
where the time goes:
time: 183 us
  waiting for transfers between devices  59.3 us (32%)
  Pallas kernels  49.3 us (27%)
  starting transfers between devices  42.7 us (23%)
  local copies, waits for them, and re-layouts  22.2 us (12%)
  other arithmetic  7.7 us (4%)
    ppermute x36, waiting for transfers between devices, xor_permute(): return lax.ppermute(values, 'dp', [(i, i ^ 1 << bit) for i in range(size)])  59.3 us
    pallas_call x8, Pallas kernels, call(): pl.pallas_call(body, name=name, out_shape=shapes, in_specs=in_specs, out_...  49.3 us
    ppermute x36, starting transfers between devices, xor_permute(): return lax.ppermute(values, 'dp', [(i, i ^ 1 << bit) for i in range(size)])  42.7 us
    unnamed x116, local copies, waits for them, and re-layouts  20.9 us
  transfers between devices with their start and end apart: 36, of which 20 were waited for; matrix products, arithmetic and copies ran while one was open for 4% of the time, Pallas kernels for 18%

commit v1 on v0

v1 whole, which is shorter than its diff:
```python
import functools
import math

import jax
import jax.numpy as jnp
from jax import lax
from jax.experimental import pallas as pl
from jax.experimental.pallas import tpu as pltpu
from jax.sharding import PartitionSpec as P

D = 384
FF = 1536
HEADS = 6
HEAD_DIM = 64
SEQ = 197
MICRO = 2
STEP = 10
P_SIZE = 1774080

LANES = 128
ROWS = 208
TOKENS = MICRO * ROWS
PAIRS = HEADS // 2
COST = 1
VMEM_LIMIT = 10 * 1024 * 1024
BLOCK = 512

eps_norm = 1e-06
beta_one = 0.9
beta_two = 0.999
adam_eps = 1e-08
rate_matrix = 0.1
rate_vector = 0.5
decay_matrix = 0.05
sqrt_half = 0.7071067811865476
inverse_root_tau = 0.3989422804014327

f32 = jnp.float32
bf16 = jnp.bfloat16


def layout():
    return [
        ("ln1_gain", (D,)),
        ("ln1_shift", (D,)),
        ("w_qkv", (D, 3 * D)),
        ("bias_query", (D,)),
        ("bias_value", (D,)),
        ("w_attn_out", (D, D)),
        ("bias_attn_out", (D,)),
        ("ln2_gain", (D,)),
        ("ln2_shift", (D,)),
        ("w_lift", (D, FF)),
        ("bias_lift", (FF,)),
        ("w_drop", (FF, D)),
        ("bias_drop", (D,)),
    ]


def row_offsets():
    offsets, at = {}, 0
    for label, shape in layout():
        offsets[label] = at
        at += math.prod(shape) // LANES
    offsets["end"] = at
    return offsets


ROW = row_offsets()
MLP_ROW = ROW["ln2_gain"]


def matrix_flags(position):
    square = D * D
    lifted = D * FF
    bounds = [
        (2 * D, 2 * D + 3 * square),
        (4 * D + 3 * square, 4 * D + 4 * square),
        (7 * D + 4 * square, 7 * D + 4 * square + lifted),
        (7 * D + 4 * square + lifted + FF, 7 * D + 4 * square + 2 * lifted + FF),
    ]
    flags = jnp.zeros(position.shape, dtype=bool)
    for lower, upper in bounds:
        flags = flags | (position >= lower) & (position < upper)
    return flags


def round_up(value, step):
    return (value + step - 1) // step * step


def dot(a, b, dims):
    return lax.dot_general(a, b, ((dims[0], dims[1]), ((), ())), preferred_element_type=f32)


def dot_nn(a, b):
    return dot(a, b, ((1,), (0,)))


def dot_nt(a, b):
    return dot(a, b, ((1,), (1,)))


def dot_tn(a, b):
    return dot(a, b, ((0,), (0,)))


def read_vector(flat, row, count):
    parts = [flat[row + i : row + i + 1, :] for i in range(count)]
    return jnp.concatenate(parts, axis=1)


def write_vector(flat, row, values):
    for i in range(values.shape[1] // LANES):
        flat[row + i : row + i + 1, :] = values[:, i * LANES : (i + 1) * LANES]


def read_matrix(flat, row, out, depth, width):
    blocks = width // LANES
    for j in range(blocks):
        part = flat[pl.ds(row + j, depth, stride=blocks), :]
        out[:, j * LANES : (j + 1) * LANES] = part.astype(bf16)


def write_matrix(flat, row, values, blocks):
    depth, width = values.shape
    for j in range(width // LANES):
        flat[pl.ds(row + j, depth, stride=blocks), :] = values[:, j * LANES : (j + 1) * LANES]


def normalize(values):
    center = values - jnp.mean(values, -1, keepdims=True)
    rstd = lax.rsqrt(jnp.mean(center * center, -1, keepdims=True) + eps_norm)
    return center * rstd, rstd


def norm_back(incoming, unit, rstd, gain):
    scaled = incoming * gain
    inner = jnp.mean(scaled * unit, -1, keepdims=True)
    back = rstd * (scaled - jnp.mean(scaled, -1, keepdims=True) - unit * inner)
    gain_grad = jnp.sum(incoming * unit, 0, keepdims=True)
    return back, gain_grad, jnp.sum(incoming, 0, keepdims=True)


def head_mask(head):
    lane = lax.broadcasted_iota(jnp.int32, (1, LANES), 1)
    return lane < HEAD_DIM if head == 0 else lane >= HEAD_DIM


def pair_slices(step):
    image, pair = step // PAIRS, step % PAIRS
    rows = pl.ds(pl.multiple_of(image * ROWS, 16), ROWS)
    cols = [pl.ds(pl.multiple_of(t * D + pair * LANES, LANES), LANES) for t in range(3)]
    return rows, cols


def unpack(rows_each, base, first_chunk, place, near, far, flat):
    count, padded = near.shape[0], near.shape[1]
    for chunk in range(first_chunk[0], first_chunk[1]):
        at = place[chunk]
        own = lax.rem(at, count)
        rows = jnp.where(at < count, near[own].astype(f32), far[own].astype(f32))
        begin = (first_chunk[2] + chunk) * rows_each - base
        flat[begin : begin + padded, :] = rows


def attention_forward(rows_each, first, place, near, far, state, *refs):
    if first:
        kept_state, refs = refs[0], refs[1:]
    w_qkv, w_out, vectors, normed_one, qkv, probs, mixed, hidden, flat = refs
    unpack(rows_each, 0, (0, -(-MLP_ROW // rows_each), 0), place, near, far, flat)
    read_matrix(flat, ROW["w_qkv"], w_qkv, D, 3 * D)
    read_matrix(flat, ROW["w_attn_out"], w_out, D, D)
    labels = ["ln1_gain", "ln1_shift", "bias_query", "bias_value", "bias_attn_out"]
    for at, label in enumerate(labels):
        vectors[at : at + 1, :] = read_vector(flat, ROW[label], 3)
    gain, shift = vectors[0:1, :], vectors[1:2, :]
    if first:
        kept_state[...] = jnp.zeros_like(kept_state)
        for image in range(MICRO):
            kept_state[image * ROWS : image * ROWS + SEQ, :] = state[image].astype(f32)
        x = kept_state[...]
    else:
        x = state[...]
    unit, _ = normalize(x)
    normed_one[...] = (unit * gain + shift).astype(bf16)
    bias_query = vectors[2:3, :]
    bias = jnp.concatenate([bias_query, jnp.zeros_like(bias_query), vectors[3:4, :]], axis=1)
    for t in range(3):
        cols = slice(t * D, (t + 1) * D)
        product = dot_nn(normed_one[...], w_qkv[:, cols]) + bias[:, cols]
        qkv[:, cols] = product.astype(bf16)

    def step(at, carry):
        rows, cols = pair_slices(at)
        query, key_rows, value_rows = qkv[rows, cols[0]], qkv[rows, cols[1]], qkv[rows, cols[2]]
        real = lax.broadcasted_iota(jnp.int32, (ROWS, ROWS), 1) < SEQ
        sides = []
        for head in range(2):
            own_key = jnp.where(head_mask(head), key_rows, jnp.zeros_like(key_rows))
            raw = jnp.where(real, dot_nt(query, own_key), -1e30)
            powers = jnp.exp((raw - jnp.max(raw, -1, keepdims=True)) * HEAD_DIM ** (-0.5))
            weight = powers / jnp.sum(powers, -1, keepdims=True)
            weight = weight.astype(bf16)
            probs[at * 2 + head] = weight
            sides.append(dot_nn(weight, value_rows))
        mixed[rows, pl.ds(pl.multiple_of((at % PAIRS) * LANES, LANES), LANES)] = jnp.where(
            head_mask(0), sides[0], sides[1]
        ).astype(bf16)
        return carry

    lax.fori_loop(0, MICRO * PAIRS, step, 0)
    hidden[...] = x + dot_nn(mixed[...], w_out[...]) + vectors[4:5, :]


def mlp_forward(rows_each, last, place_low, place_high, low_near, low_far, near, far, hidden, *refs):
    w_lift, w_drop, vectors, normed_two, active, slope, result, flat = refs
    count = 2 * near.shape[0]
    begin = MLP_ROW // rows_each
    base = begin * rows_each
    unpack(rows_each, base, (begin, count, 0), place_low, low_near, low_far, flat)
    unpack(rows_each, base, (0, count, count), place_high, near, far, flat)
    read_matrix(flat, ROW["w_lift"] - base, w_lift, D, FF)
    read_matrix(flat, ROW["w_drop"] - base, w_drop, FF, D)
    for at, label in enumerate(["ln2_gain", "ln2_shift", "bias_drop"]):
        vectors[at : at + 1, :] = read_vector(flat, ROW[label] - base, 3)
    bias_lift = read_vector(flat, ROW["bias_lift"] - base, FF // LANES)
    gain, shift = vectors[0:1, :], vectors[1:2, :]
    unit, _ = normalize(hidden[...])
    normed_two[...] = (unit * gain + shift).astype(bf16)
    total = hidden[...] + vectors[2:3, :]
    for at in range(0, FF, BLOCK):
        cols = slice(at, at + BLOCK)
        lifted = dot_nn(normed_two[...], w_lift[:, cols]) + bias_lift[:, cols]
        below = 0.5 * (1.0 + lax.erf(lifted * sqrt_half))
        active[:, cols] = (lifted * below).astype(bf16)
        bell = jnp.exp(-0.5 * lifted * lifted) * inverse_root_tau
        slope[:, cols] = (below + lifted * bell).astype(bf16)
        total += dot_nn(active[:, cols], w_drop[cols, :])
    if last:
        for image in range(MICRO):
            result[image] = total[image * ROWS : image * ROWS + SEQ, :]
    else:
        result[...] = total


def pack(flat, base, rows_each, first_chunk, places, near, far):
    count, padded = near.shape[1], near.shape[2]
    even = places[0][0] < count
    for parity in range(2):

        @pl.when(even if parity == 0 else jnp.logical_not(even))
        def _():
            for quarter, place in enumerate(places):
                for chunk in range(2 * count):
                    at = (first_chunk + quarter * 2 * count + chunk) * rows_each - base
                    out = near if chunk % 2 == parity else far
                    out[quarter, lax.rem(place[chunk], count)] = flat[at : at + padded, :].astype(bf16)


def mlp_backward(rows_each, last, *refs):
    if last:
        present, refs = refs[0], refs[1:]
    places, refs = refs[:2], refs[2:]
    incoming, hidden, w_lift, w_drop, vectors, normed_two, active, slope = refs[:8]
    refs = refs[8:]
    carry, near, far, g_hidden, flat = refs[:5]
    count = 4 * near.shape[1]
    if last:
        kept = refs[5]
        kept[...] = jnp.zeros_like(kept)
        for image in range(MICRO):
            seed = incoming[image].astype(f32) * present[image].astype(f32)
            kept[image * ROWS : image * ROWS + SEQ, :] = seed
        g = kept[...]
    else:
        g = incoming[...]
    base = MLP_ROW
    end = ROW["end"] - base
    flat[end:, :] = jnp.zeros((flat.shape[0] - end, LANES), f32)
    g_out = g.astype(bf16)
    write_vector(flat, ROW["bias_drop"] - base, jnp.sum(g_out.astype(f32), 0, keepdims=True))
    d_normed = jnp.zeros((TOKENS, D), f32)
    for at in range(0, FF, BLOCK):
        cols = slice(at, at + BLOCK)
        row = ROW["w_drop"] - base + at * (D // LANES)
        write_matrix(flat, row, dot_tn(active[:, cols], g_out), D // LANES)
        d_lifted = (dot_nt(g_out, w_drop[cols, :]) * slope[:, cols].astype(f32)).astype(bf16)
        row = ROW["bias_lift"] - base + at // LANES
        write_vector(flat, row, jnp.sum(d_lifted.astype(f32), 0, keepdims=True))
        row = ROW["w_lift"] - base + at // LANES
        write_matrix(flat, row, dot_tn(normed_two[...], d_lifted), FF // LANES)
        d_normed += dot_nt(d_lifted, w_lift[:, cols])
    unit, rstd = normalize(hidden[...])
    back, gain_grad, shift_grad = norm_back(d_normed, unit, rstd, vectors[0:1, :])
    write_vector(flat, ROW["ln2_gain"] - base, gain_grad)
    write_vector(flat, ROW["ln2_shift"] - base, shift_grad)
    g_hidden[...] = g + back
    carry[...] = flat[: carry.shape[0], :]
    pack(flat, base, rows_each, count, places, near, far)


def attention_backward(g_hidden, w_out, qkv, probs, mixed, d_qkv, d_out, bias_out, d_mixed):
    g_att = g_hidden[...].astype(bf16)
    bias_out[...] = jnp.broadcast_to(jnp.sum(g_att.astype(f32), 0, keepdims=True), bias_out.shape)
    d_out[...] = dot_tn(mixed[...], g_att)
    d_mixed[...] = dot_nt(g_att, w_out[...]).astype(bf16)

    def step(at, carried):
        rows, cols = pair_slices(at)
        query, key_rows, value_rows = qkv[rows, cols[0]], qkv[rows, cols[1]], qkv[rows, cols[2]]
        mixed_grad = d_mixed[rows, pl.ds(pl.multiple_of((at % PAIRS) * LANES, LANES), LANES)]
        d_query, d_key, d_value = [], [], []
        for head in range(2):
            own = jnp.where(head_mask(head), mixed_grad, jnp.zeros_like(mixed_grad))
            weight = probs[at * 2 + head]
            d_value.append(dot_tn(weight, mixed_grad))
            weight = weight.astype(f32)
            d_probs = dot_nt(own, value_rows)
            inner = jnp.sum(weight * d_probs, -1, keepdims=True)
            d_scores = (weight * (d_probs - inner)).astype(bf16)
            d_query.append(dot_nn(d_scores, key_rows))
            d_key.append(dot_tn(d_scores, query))
        scale = HEAD_DIM ** (-0.5)
        mask = head_mask(0)
        d_qkv[rows, cols[0]] = (jnp.where(mask, d_query[0], d_query[1]) * scale).astype(bf16)
        d_qkv[rows, cols[1]] = (jnp.where(mask, d_key[0], d_key[1]) * scale).astype(bf16)
        d_qkv[rows, cols[2]] = jnp.where(mask, d_value[0], d_value[1]).astype(bf16)
        return carried

    lax.fori_loop(0, MICRO * PAIRS, step, 0)

def projection_backward(rows_each, first, *refs):
    places, refs = refs[:2], refs[2:]
    g_hidden, state, w_qkv, vectors, normed_one, d_qkv, d_out, bias_out, carry = refs[:9]
    near, far, input_grad, flat = refs[9:]
    flat[MLP_ROW : MLP_ROW + carry.shape[0], :] = carry[...]
    write_vector(flat, ROW["bias_attn_out"], bias_out[0:1, :])
    write_matrix(flat, ROW["w_attn_out"], d_out[...], D // LANES)
    query_sum = jnp.sum(d_qkv[:, :D].astype(f32), 0, keepdims=True)
    write_vector(flat, ROW["bias_query"], query_sum)
    value_sum = jnp.sum(d_qkv[:, 2 * D :].astype(f32), 0, keepdims=True)
    write_vector(flat, ROW["bias_value"], value_sum)
    d_normed = jnp.zeros((TOKENS, D), f32)
    for t in range(3):
        cols = slice(t * D, (t + 1) * D)
        part = d_qkv[:, cols]
        row = ROW["w_qkv"] + t * (D // LANES)
        write_matrix(flat, row, dot_tn(normed_one[...], part), 3 * D // LANES)
        d_normed += dot_nt(part, w_qkv[:, cols])
    unit, rstd = normalize(state[...])
    back, gain_grad, shift_grad = norm_back(d_normed, unit, rstd, vectors[0:1, :])
    write_vector(flat, ROW["ln1_gain"], gain_grad)
    write_vector(flat, ROW["ln1_shift"], shift_grad)
    total = g_hidden[...] + back
    if first:
        for image in range(MICRO):
            input_grad[image] = total[image * ROWS : image * ROWS + SEQ, :]
    else:
        input_grad[...] = total
    pack(flat, 0, rows_each, 0, places, near, far)


def call(body, name, inputs, outputs, scratch, scalars=0, flops=0):
    in_specs = [pl.BlockSpec(memory_space=pltpu.SMEM)] * scalars
    in_specs += [pl.BlockSpec(memory_space=pltpu.VMEM)] * (len(inputs) - scalars)
    shapes = [jax.ShapeDtypeStruct(shape, dtype) for shape, dtype in outputs]
    moved = sum(math.prod(s.shape) * s.dtype.itemsize for s in list(inputs) + shapes)
    return pl.pallas_call(
        body,
        name=name,
        out_shape=shapes,
        in_specs=in_specs,
        out_specs=[pl.BlockSpec(memory_space=pltpu.VMEM)] * len(shapes),
        scratch_shapes=scratch,
        compiler_params=pltpu.CompilerParams(vmem_limit_bytes=VMEM_LIMIT),
        cost_estimate=pl.CostEstimate(flops=flops // COST, bytes_accessed=moved // COST, transcendentals=0),
    )(*inputs)


def tie(values, *before):
    return lax.optimization_barrier((values, before))[0]


def together(*values):
    return lax.optimization_barrier(values)


def swap(values, size, mask):
    return lax.ppermute(values, "dp", [(i, i ^ mask) for i in range(size)])


def gather_masks(bits):
    chain = [1 << bit for bit in range(bits - 2, 2, -1)]
    return [chain + [2, 4, 1], chain + [4, 2, 1]]


def places(me, size, masks):
    relative = me ^ jnp.arange(size // 2, dtype=jnp.int32)
    place = jnp.zeros_like(relative)
    for digit, mask in enumerate(masks):
        place = place | jnp.where(relative & mask != 0, 1 << digit, 0)
    return place


def sent(part, size, mask):
    middle = part.shape[0] // 2
    return part[:middle], swap(part[middle:], size, mask)


def added(pair):
    return (pair[0].astype(f32) + pair[1].astype(f32)).astype(bf16)


def shards(size, images, cotangent, present, params, first_moment, second_moment):
    bits = size.bit_length() - 1
    width = params.shape[1]
    rows_each = width // LANES
    padded = round_up(rows_each, 16)
    half = size // 2
    me = lax.axis_index("dp")
    chain = [1 << bit for bit in range(bits - 2, 2, -1)]
    planes = [(2, 4), (4, 2)]
    place_low, place_high = [places(me, size, chain + [mask, 6 - mask, 1]) for mask in planes[0]]
    place = [places(me, size // 2, chain[1:] + [mask, 6 - mask, 1]) for mask in planes[0]]

    is_low, is_first = (me >> (bits - 1)) & 1 == 0, (me >> (bits - 2)) & 1 == 0
    flags = matrix_flags(me * width + jnp.arange(width, dtype=jnp.int32)).astype(f32)
    early = together(params, is_low, is_first, flags, place_low, place_high, *place)
    params, is_low, is_first, flags, place_low, place_high, *place = early
    compact = params.astype(bf16).reshape(2, rows_each, LANES)
    compact = jnp.pad(compact, ((0, 0), (0, padded - rows_each), (0, 0)))

    low_flat = pltpu.VMEM((-(-MLP_ROW // rows_each) * rows_each + padded, LANES), f32)
    begin = MLP_ROW // rows_each
    high_flat = pltpu.VMEM(((size - begin) * rows_each + padded, LANES), f32)
    square = TOKENS * D * D
    core_flops = 2 * 2 * MICRO * HEADS * ROWS * ROWS * HEAD_DIM

    def attend(first, near, far, state):
        outputs = [((TOKENS, D), f32)] if first else []
        outputs += [
            ((D, 3 * D), bf16),
            ((D, D), bf16),
            ((8, D), f32),
            ((TOKENS, D), bf16),
            ((TOKENS, 3 * D), bf16),
            ((MICRO * HEADS, ROWS, ROWS), bf16),
            ((TOKENS, D), bf16),
            ((TOKENS, D), f32),
        ]
        made = call(
            functools.partial(attention_forward, rows_each, first),
            "attention_forward",
            [place_low, near, far, state],
            outputs,
            [low_flat],
            scalars=1,
            flops=8 * square + core_flops,
        )
        made = made if first else [state, *made]
        return made[:-1], made[-1]

    def lift(last, low_near, low_far, near, far, hidden):
        made = call(
            functools.partial(mlp_forward, rows_each, last),
            "mlp_forward",
            [place_low, place_high, low_near, low_far, near, far, hidden],
            [
                ((D, FF), bf16),
                ((FF, D), bf16),
                ((8, D), f32),
                ((TOKENS, D), bf16),
                ((TOKENS, FF), bf16),
                ((TOKENS, FF), bf16),
                ((MICRO, SEQ, D) if last else (TOKENS, D), f32),
            ],
            [high_flat],
            scalars=2,
            flops=16 * square,
        )
        return (hidden, *made[:-1]), made[-1]

    grads_shape = ((2, size // 8, padded, LANES), bf16)

    def lift_back(last, incoming, kept):
        scratch = [pltpu.VMEM((size * rows_each + padded - MLP_ROW, LANES), f32)]
        if last:
            scratch.append(pltpu.VMEM((TOKENS, D), f32))
        return call(
            functools.partial(mlp_backward, rows_each, last),
            "mlp_backward",
            ([present] if last else []) + [*place, incoming, *kept],
            [((carry_rows, LANES), f32), grads_shape, grads_shape, ((TOKENS, D), f32)],
            scratch,
            scalars=3 if last else 2,
            flops=32 * square,
        )

    def attend_back(g_hidden, kept):
        state, w_qkv, w_out, vectors, normed_one, qkv, probs, mixed = kept
        return call(
            attention_backward,
            "attention_backward",
            [g_hidden, w_out, qkv, probs, mixed],
            [((TOKENS, 3 * D), bf16), ((D, D), f32), ((8, D), f32)],
            [pltpu.VMEM((TOKENS, D), bf16)],
            flops=4 * square + 2 * core_flops,
        )

    def project_back(first, g_hidden, kept, *made):
        state, w_qkv, w_out, vectors, normed_one, qkv, probs, mixed = kept
        return call(
            functools.partial(projection_backward, rows_each, first),
            "projection_backward",
            [*place, g_hidden, state, w_qkv, vectors, normed_one, *made],
            [grads_shape, grads_shape, ((MICRO, SEQ, D) if first else (TOKENS, D), f32)],
            [pltpu.VMEM((MLP_ROW + carry_rows, LANES), f32)],
            scalars=2,
            flops=12 * square,
        )

    def top_gathered(shard, other):
        return jnp.stack([jnp.where(is_low, shard, other), jnp.where(is_low, other, shard)])[None]

    def moved(parts, step):
        return [swap(part, size, mask) for part, mask in zip(parts, planes[step])]

    def joined(parts, received):
        return [jnp.concatenate(pair) for pair in zip(parts, received)]

    def chained(chunks):
        for mask in chain[:-1]:
            chunks = jnp.concatenate([chunks, swap(chunks, size, mask)])
        return chunks, swap(chunks, size, chain[-1])

    def halved(chunks, received):
        chunks = jnp.concatenate([chunks, received])
        return chunks[:, 0], chunks[:, 1]

    top0 = top_gathered(compact[0], swap(compact[0], size, size // 2))
    half0 = halved(*chained(top0))
    received0 = moved(half0, 0)
    row1, *received0 = together(compact[1], *received0)
    half0 = joined(half0, received0)
    received0 = moved(half0, 1)
    chunks1, received1 = chained(top_gathered(row1, swap(row1, size, size // 2)))
    *received0, received1 = together(*received0, received1)
    near0 = joined(half0, received0)
    half1 = halved(chunks1, received1)
    far0 = [swap(part, size, 1) for part in near0]
    received1 = moved(half1, 0)
    *far0, received1[0], received1[1] = together(*far0, *received1)
    half1 = joined(half1, received1)
    received1 = moved(half1, 1)
    one0, hidden = attend(True, near0[0], far0[0], images)
    hidden, *received1 = together(hidden, *received1)
    near1 = joined(half1, received1)
    far1 = [swap(part, size, 1) for part in near1]
    two0, state = lift(False, near0[0], far0[0], near0[1], far0[1], hidden)
    state, *far1 = together(state, *far1)
    one1, hidden = attend(False, near1[0], far1[0], state)
    two1, outputs = lift(True, near1[0], far1[0], near1[1], far1[1], hidden)

    carry_rows = round_up(half * rows_each - MLP_ROW + padded - rows_each, 8)

    def to_plane(pairs, step):
        return [sent(added(pair), size, mask) for pair, mask in zip(pairs, planes[step])]

    def to_core(near, far):
        received = swap(far, size, 1)
        return [(near[quarter], received[quarter]) for quarter in range(2)]

    def along(pairs):
        parts = [added(pair) for pair in pairs]
        for mask in reversed(chain[1:]):
            parts = [added(sent(part, size, mask)) for part in parts]
        return parts

    def hold(pairs, *others):
        values = together(*[value for pair in pairs for value in pair], *others)
        count = 2 * len(pairs)
        return [values[i : i + 2] for i in range(0, count, 2)], *values[count:]

    def to_inner(low, high):
        kept = jnp.concatenate([jnp.where(is_first, *part) for part in (low, high)])
        given = jnp.concatenate([jnp.where(is_first, *part[::-1]) for part in (low, high)])
        return kept, swap(given, size, size // 4)

    def to_top(halves):
        kept = jnp.where(is_low, halves[0], halves[1])
        return kept, swap(jnp.where(is_low, halves[1], halves[0]), size, size // 2)

    carry, near, far, g_hidden = lift_back(True, cotangent, two1)
    high1 = to_core(near, far)
    made = attend_back(g_hidden, one1)
    high1, *made = hold(high1, *made)
    near, far, incoming = project_back(False, g_hidden, one1, *made, carry)
    high1 = to_plane(high1, 1)
    low1 = to_core(near, far)
    carry, near, far, g_hidden = lift_back(False, incoming, two0)
    held, g_hidden = hold(high1 + low1, g_hidden)
    high1, low1 = to_plane(held[:2], 0), to_plane(held[2:], 1)
    high0 = to_core(near, far)
    made = attend_back(g_hidden, one0)
    held, *made = hold(high1 + low1 + high0, *made)
    high1, low1, high0 = along(held[:2]), to_plane(held[2:4], 0), to_plane(held[4:], 1)
    near, far, input_grad = project_back(True, g_hidden, one0, *made, carry)
    low0 = to_core(near, far)
    held, = hold(low0 + low1 + high0)
    low0, low1, high0 = to_plane(held[:2], 1), along(held[2:4]), to_plane(held[4:], 0)
    inner1 = to_inner(low1, high1)
    held, = hold(low0 + high0 + [inner1])
    low0, high0, inner1 = to_plane(held[:2], 0), along(held[2:4]), added(held[4])
    top1 = to_top(inner1)
    held, = hold(low0 + [top1])
    low0, top1 = along(held[:2]), held[2]
    top0 = to_top(added(to_inner(low0, high0)))
    sum0, sum1 = [pair[0].astype(f32) + pair[1].astype(f32) for pair in (top0, top1)]
    owned = [total[:rows_each].reshape(width) for total in (sum0, sum1)]

    grads = jnp.stack(owned)
    flags = flags[None, :] > 0
    rate = jnp.where(flags, rate_matrix, rate_vector)
    decay = jnp.where(flags, decay_matrix, 0.0)
    new_first = beta_one * first_moment + (1.0 - beta_one) * grads
    new_second = beta_two * second_moment + (1.0 - beta_two) * grads * grads
    first_hat = new_first / (1.0 - beta_one**STEP)
    second_hat = new_second / (1.0 - beta_two**STEP)
    new_params = params - rate * (first_hat / (jnp.sqrt(second_hat) + adam_eps) + decay * params)
    return (outputs, input_grad, new_params, new_first, new_second)


def solution(mesh):
    in_specs = (
        P("dp", None, None),
        P("dp", None, None),
        P("dp"),
        P(None, "dp"),
        P(None, "dp"),
        P(None, "dp"),
    )
    out_specs = (
        P("dp", None, None),
        P("dp", None, None),
        P(None, "dp"),
        P(None, "dp"),
        P(None, "dp"),
    )
    body = functools.partial(shards, mesh.shape["dp"])
    return jax.shard_map(body, mesh=mesh, in_specs=in_specs, out_specs=out_specs, check_vma=False)
```

time: 183 us -> 166 us (0.907)
  local copies, waits for them, and re-layouts: 22.2 us -> 4.33 us
    unnamed x116 -> x18, local copies, waits for them, and re-layouts: 20.9 us -> 3.05 us
    ppermute x36 -> x40, starting transfers between devices: 42.7 us -> 44.3 us  [swap(): return lax.ppermute(values, 'dp', [(i, i ^ mask) for i in range(size)])]
    pallas_call x8 -> x10, Pallas kernels: 49.3 us -> 50 us  [call(): pl.pallas_call(body, name=name, out_shape=shapes, in_specs=in_specs, out_...]
    ppermute x36 -> x40, waiting for transfers between devices: 59.3 us -> 58.8 us  [swap(): return lax.ppermute(values, 'dp', [(i, i ^ mask) for i in range(size)])]
  transfers between devices with their start and end apart: 36 -> 40, of which waited for: 20 -> 20; matrix products, arithmetic and copies ran while one was open for 4% -> 3% of each run, Pallas kernels for 18% -> 19%
where the time goes in v1:
time: 166 us
  waiting for transfers between devices  58.8 us (35%)
  Pallas kernels  50 us (30%)
  starting transfers between devices  44.3 us (27%)
  other arithmetic  7.14 us (4%)
  local copies, waits for them, and re-layouts  4.33 us (3%)
    ppermute x40, waiting for transfers between devices, swap(): return lax.ppermute(values, 'dp', [(i, i ^ mask) for i in range(size)])  58.8 us
    pallas_call x10, Pallas kernels, call(): pl.pallas_call(body, name=name, out_shape=shapes, in_specs=in_specs, out_...  50 us
    ppermute x40, starting transfers between devices, swap(): return lax.ppermute(values, 'dp', [(i, i ^ mask) for i in range(size)])  44.3 us
  transfers between devices with their start and end apart: 40, of which 20 were waited for; matrix products, arithmetic and copies ran while one was open for 3% of the time, Pallas kernels for 19%

profile of v1, /device:TPU:0, one launch (start us, length us, event | category | flops | bytes accessed | tf_op | source)
XLA Modules:
  0.0 166.0 jit_solution(10121730415949016057)
XLA Ops:
  2.5 4.1 %collective-permute-start = (bf16[448,128]{1,0:T(8,128)(2,1)S(1)}, bf16[448,128]{1,0:T(8,128)(2,1)S(1)}, u32[]{:S(2)}, u32[]{:S(2)}) collective-permute-start(bf16[448,128]{1,0:T(8,128)(2,1)S(1)} %get-tuple-element.356), channel_id=1, source_target_pairs={{0,16},{1,17},{2,18},{3,19},{4,20},{5,21},{6,22},{7,23},{8,24},{9,... | collective-permute-start | bytes 344072 | tf_op jit(solution)/shard_map/ppermute | solution.py:390
  6.6 5.6 %collective-permute-done = bf16[448,128]{1,0:T(8,128)(2,1)S(1)} collective-permute-done((bf16[448,128]{1,0:T(8,128)(2,1)S(1)}, bf16[448,128]{1,0:T(8,128)(2,1)S(1)}, u32[]{:S(2)}, u32[]{:S(2)}) %collective-permute-start) | collective-permute-done | bytes 114720 | tf_op jit(solution)/shard_map/ppermute | solution.py:390
  13.1 6.1 %collective-permute-done.1 = bf16[1,2,448,128]{3,2,1,0:T(8,128)(2,1)S(1)} collective-permute-done((bf16[1,2,448,128]{3,2,1,0:T(8,128)(2,1)S(1)}, bf16[1,2,448,128]{3,2,1,0:T(8,128)(2,1)S(1)}, u32[]{:S(2)}, u32[]{:S(2)}) %collective-permute-start.1) | collective-permute-done | bytes 229408 | tf_op jit(solution)/shard_map/ppermute | solution.py:390
  22.0 3.3 %collective-permute-done.2 = bf16[2,448,128]{2,1,0:T(8,128)(2,1)S(1)} collective-permute-done((bf16[2,448,128]{2,1,0:T(8,128)(2,1)S(1)}, bf16[2,448,128]{2,1,0:T(8,128)(2,1)S(1)}, u32[]{:S(2)}, u32[]{:S(2)}) %collective-permute-start.2) | collective-permute-done | bytes 229408 | tf_op jit(solution)/shard_map/ppermute | solution.py:390
  28.1 4.0 %collective-permute-start.4 = (bf16[448,128]{1,0:T(8,128)(2,1)S(1)}, bf16[448,128]{1,0:T(8,128)(2,1)S(1)}, u32[]{:S(2)}, u32[]{:S(2)}) collective-permute-start(bf16[448,128]{1,0:T(8,128)(2,1)S(1)} %get-tuple-element.143), channel_id=1, source_target_pairs={{0,16},{1,17},{2,18},{3,19},{4,20},{5,21},{6,22},{7,23},{8,24},{9,... | collective-permute-start | bytes 344072 | tf_op jit(solution)/shard_map/ppermute | solution.py:390
  32.8 3.4 %collective-permute-done.4 = bf16[448,128]{1,0:T(8,128)(2,1)S(1)} collective-permute-done((bf16[448,128]{1,0:T(8,128)(2,1)S(1)}, bf16[448,128]{1,0:T(8,128)(2,1)S(1)}, u32[]{:S(2)}, u32[]{:S(2)}) %collective-permute-start.4) | collective-permute-done | bytes 114720 | tf_op jit(solution)/shard_map/ppermute | solution.py:390
  37.3 5.1 %collective-permute-done.7 = bf16[1,2,448,128]{3,2,0,1:T(8,128)(2,1)S(1)} collective-permute-done((bf16[1,2,448,128]{3,2,0,1:T(8,128)(2,1)S(1)}, bf16[1,2,448,128]{3,2,0,1:T(8,128)(2,1)S(1)}, u32[]{:S(2)}, u32[]{:S(2)}) %collective-permute-start.7) | collective-permute-done | bytes 229408 | tf_op jit(solution)/shard_map/ppermute | solution.py:390
  44.5 6.5 %collective-permute-done.10 = bf16[2,448,128]{2,1,0:T(8,128)(2,1)S(1)} collective-permute-done((bf16[2,448,128]{2,1,0:T(8,128)(2,1)S(1)}, bf16[2,448,128]{2,1,0:T(8,128)(2,1)S(1)}, u32[]{:S(2)}, u32[]{:S(2)}) %collective-permute-start.10) | collective-permute-done | bytes 229408 | tf_op jit(solution)/shard_map/ppermute | solution.py:390
  53.4 7.9 %attention_forward.2 = (f32[416,384]{1,0:T(8,128)S(1)}, bf16[384,1152]{1,0:T(8,128)(2,1)S(1)}, bf16[384,384]{1,0:T(8,128)(2,1)S(1)}, f32[8,384]{1,0:T(8,128)S(1)...) custom-call(s32[16]{0:T(128)S(1)} %get-tuple-element.139.place.place, ...), custom_call_target="tpu_custom_call" | custom-call | flops 623640576 | bytes 7243328 | tf_op jit(solution)/shard_map/attention_forward/pallas_call | solution.py:369
  64.1 4.1 %mlp_forward.2 = (bf16[384,1536]{1,0:T(8,128)(2,1)S(1)}, bf16[1536,384]{1,0:T(8,128)(2,1)S(1)}, f32[8,384]{1,0:T(8,128)S(1)}, bf16[416,384]{1,0:T(8,128)(2,1)S(1...) custom-call(s32[16]{0:T(128)S(1)} %get-tuple-element.139.place.place_low, ...), custom_call_target="tpu_custom_call" | custom-call | flops 981467136 | bytes 10195072 | tf_op jit(solution)/shard_map/mlp_forward/pallas_call | solution.py:369
  68.2 7.7 %attention_forward.3 = (bf16[384,1152]{1,0:T(8,128)(2,1)S(1)}, bf16[384,384]{1,0:T(8,128)(2,1)S(1)}, f32[8,384]{1,0:T(8,128)S(1)}, bf16[416,384]{1,0:T(8,128)(2,...) custom-call(s32[16]{0:T(128)S(1)} %get-tuple-element.139.place.place, ...), custom_call_target="tpu_custom_call" | custom-call | flops 623640576 | bytes 6940736 | tf_op jit(solution)/shard_map/attention_forward/pallas_call | solution.py:369
  76.0 4.1 %mlp_forward.3 = (bf16[384,1536]{1,0:T(8,128)(2,1)S(1)}, bf16[1536,384]{1,0:T(8,128)(2,1)S(1)}, f32[8,384]{1,0:T(8,128)S(1)}, bf16[416,384]{1,0:T(8,128)(2,1)S(1...) custom-call(s32[16]{0:T(128)S(1)} %get-tuple-element.139.place.place_low, ...), custom_call_target="tpu_custom_call" | custom-call | flops 981467136 | bytes 10161280 | tf_op jit(solution)/shard_map/mlp_forward/pallas_call | solution.py:369
  80.1 4.5 %mlp_backward.2 = (f32[2336,128]{1,0:T(8,128)S(1)}, bf16[2,4,448,128]{3,2,1,0:T(8,128)(2,1)S(1)}, bf16[2,4,448,128]{3,2,1,0:T(8,128)(2,1)S(1)}, f32[416,384]{1,0:T(8,128)S(1)}) custom-call(s32[2]{0:T(128)S(1)} %copy-done, s32[8]{0:T(128)S(1)} %get-tuple-element.163.refs_1_.refs_0_, s32[8]{0:T(128)S(1)} %get-tuple-element.164.refs_2_.refs_1_, ...), custom_call_target="tpu_custom_call" | custom-call | flops 1962934272 | bytes 9858632 | tf_op jit(solution)/shard_map/mlp_backward/pallas_call | solution.py:369
  84.8 6.0 %attention_backward.2 = (bf16[416,1152]{1,0:T(8,128)(2,1)S(1)}, f32[384,384]{1,0:T(8,128)S(1)}, f32[8,384]{1,0:T(8,128)S(1)}) custom-call(f32[416,384]{1,0:T(8,128)S(1)} %get-tuple-element.173.g_hidden.refs_2_, bf16[384,384]{1,0:T(8,128)(2,1)S(1)} %get-tuple-element.174.w_out, bf16[416,1152]{1,0:T(8,128)(2,1)S(1)} %get-tuple-element.175.qkv, ...), custom_call_target="tpu_custom_call" | custom-call | flops 511180800 | bytes 4810752 | tf_op jit(solution)/shard_map/attention_backward/pallas_call | solution.py:369
  97.2 4.3 %mlp_backward.3 = (f32[2336,128]{1,0:T(8,128)S(1)}, bf16[2,4,448,128]{3,2,1,0:T(8,128)(2,1)S(1)}, bf16[2,4,448,128]{3,2,1,0:T(8,128)(2,1)S(1)}, f32[416,384]{1,0:T(8,128)S(1)}) custom-call(s32[8]{0:T(128)S(1)} %get-tuple-element.163.refs_1_.refs_0_, s32[8]{0:T(128)S(1)} %get-tuple-element.164.refs_2_.refs_1_, f32[416,384]{1,0:T(8,128)S(1)} %get-tuple-element.194.refs_2_, ...), custom_call_target="tpu_custom_call" | custom-call | flops 1962934272 | bytes 10195008 | tf_op jit(solution)/shard_map/mlp_backward/pallas_call | solution.py:369
  108.4 6.0 %attention_backward.3 = (bf16[416,1152]{1,0:T(8,128)(2,1)S(1)}, f32[384,384]{1,0:T(8,128)S(1)}, f32[8,384]{1,0:T(8,128)S(1)}) custom-call(f32[416,384]{1,0:T(8,128)S(1)} %get-tuple-element.202.g_hidden.refs_2_, bf16[384,384]{1,0:T(8,128)(2,1)S(1)} %get-tuple-element.217.w_out, bf16[416,1152]{1,0:T(8,128)(2,1)S(1)} %get-tuple-element.218.qkv, ...), custom_call_target="tpu_custom_call" | custom-call | flops 511180800 | bytes 4810752 | tf_op jit(solution)/shard_map/attention_backward/pallas_call | solution.py:369
  114.5 2.7 %projection_backward.3 = (bf16[2,4,448,128]{3,2,1,0:T(8,128)(2,1)S(1)}, bf16[2,4,448,128]{3,2,1,0:T(8,128)(2,1)S(1)}, f32[2,197,384]{2,1,0:T(8,128)S(1)}) custom-call(s32[8]{0:T(128)S(1)} %get-tuple-element.163.refs_1_.refs_0_, s32[8]{0:T(128)S(1)} %get-tuple-element.164.refs_2_.refs_1_, f32[416,384]{1,0:T(8,128)S(1)} %get-tuple-element.202.g_hidden.refs_2_, ...), custom_call_target="tpu_custom_call" | custom-call | flops 736100352 | bytes 7691328 | tf_op jit(solution)/shard_map/projection_backward/pallas_call | solution.py:369
  125.1 4.2 %collective-permute-done.28 = bf16[2,448,128]{2,1,0:T(8,128)(2,1)S(1)} collective-permute-done((bf16[2,448,128]{2,1,0:T(8,128)(2,1)S(1)}, bf16[2,448,128]{2,1,0:T(8,128)(2,1)S(1)}, u32[]{:S(2)}, u32[]{:S(2)}) %collective-permute-start.28) | collective-permute-done | bytes 229408 | tf_op jit(solution)/shard_map/ppermute | solution.py:390
  135.4 3.9 %collective-permute-done.32 = bf16[1,448,128]{2,1,0:T(8,128)(2,1)S(1)} collective-permute-done((bf16[1,448,128]{2,1,0:T(8,128)(2,1)S(1)}, bf16[1,448,128]{2,1,0:T(8,128)(2,1)S(1)}, u32[]{:S(2)}, u32[]{:S(2)}) %collective-permute-start.32) | collective-permute-done | bytes 114720 | tf_op jit(solution)/shard_map/ppermute | solution.py:390
  141.9 2.6 %collective-permute-start.37 = (bf16[448,128]{1,0:T(8,128)(2,1)S(1)}, bf16[448,128]{1,0:T(8,128)(2,1)S(1)}, u32[]{:S(2)}, u32[]{:S(2)}) collective-permute-start(bf16[448,128]{1,0:T(8,128)(2,1)S(1)} %get-tuple-element.336), channel_id=1, source_target_pairs={{0,16},{1,17},{2,18},{3,19},{4,20},{5,21},{6,22},{7,23},{8,24},{9,... | collective-permute-start | bytes 344072 | tf_op jit(solution)/shard_map/ppermute | solution.py:390
  145.2 3.7 %collective-permute-done.37 = bf16[448,128]{1,0:T(8,128)(2,1)S(1)} collective-permute-done((bf16[448,128]{1,0:T(8,128)(2,1)S(1)}, bf16[448,128]{1,0:T(8,128)(2,1)S(1)}, u32[]{:S(2)}, u32[]{:S(2)}) %collective-permute-start.37) | collective-permute-done | bytes 114720 | tf_op jit(solution)/shard_map/ppermute | solution.py:390
  151.9 4.5 %collective-permute-done.38 = bf16[2,448,128]{2,1,0:T(8,128)(2,1)S(1)} collective-permute-done((bf16[2,448,128]{2,1,0:T(8,128)(2,1)S(1)}, bf16[2,448,128]{2,1,0:T(8,128)(2,1)S(1)}, u32[]{:S(2)}, u32[]{:S(2)}) %collective-permute-start.38) | collective-permute-done | bytes 229408 | tf_op jit(solution)/shard_map/ppermute | solution.py:390
  158.6 4.2 %collective-permute-done.39 = bf16[448,128]{1,0:T(8,128)(2,1)S(1)} collective-permute-done((bf16[448,128]{1,0:T(8,128)(2,1)S(1)}, bf16[448,128]{1,0:T(8,128)(2,1)S(1)}, u32[]{:S(2)}, u32[]{:S(2)}) %collective-permute-start.39) | collective-permute-done | bytes 114720 | tf_op jit(solution)/shard_map/ppermute | solution.py:390
  163.1 2.8 %multiply_subtract_fusion = (f32[2,55552]{1,0:T(2,128)}, f32[2,55552]{1,0:T(2,128)}, f32[2,55552]{1,0:T(2,128)}) fusion(f32[2,55552]{1,0:T(2,128)S(1)} %copy-done.1, f32[55552]{0:T(1024)S(1)} %broadcast_select_fusion.8, f32[55552]{0:T(1024)S(1)} %get-tuple-element.286, f32[1,55552]{1,0:T(1,128)S(1)} %bitcast.81, f32[1,55552]{1,0:T(1,128)S(1)} %bitcast.82, ...), kind=kLoop, calls=%fused_computation.49 | loop fusion | flops 1777664 | bytes 3555328 | tf_op jit(solution)/shard_map/sub | solution.py:630
  (160 shorter events, 53.1 us)
Async XLA Ops:
  2.5 9.7 %collective-permute-start = (bf16[448,128]{1,0:T(8,128)(2,1)S(1)}, bf16[448,128]{1,0:T(8,128)(2,1)S(1)}, u32[]{:S(2)}, u32[]{:S(2)}) collective-permute-start(bf16[448,128]{1,0:T(8,128)(2,1)S(1)} %get-tuple-element.356), channel_id=1, source_target_pairs={{0,16},{1,17},{2,18},{3,19},{4,20},{5,21},{6,22},{7,23},{8,24},{9,... | collective-permute-start | bytes 344072 | tf_op jit(solution)/shard_map/ppermute | solution.py:390
  12.3 6.9 %collective-permute-start.1 = (bf16[1,2,448,128]{3,2,1,0:T(8,128)(2,1)S(1)}, bf16[1,2,448,128]{3,2,1,0:T(8,128)(2,1)S(1)}, u32[]{:S(2)}, u32[]{:S(2)}) collective-permute-start(bf16[1,2,448,128]{3,2,1,0:T(8,128)(2,1)S(1)} %maximum_bitcast_fusion), channel_id=1, source_target_pairs={{0,8},{1,9},{2,10},{3,11},{4,12},{5,13},{6,14},{7,15},{8,0},{9,1},... | collective-permute-start | bytes 688136 | tf_op jit(solution)/shard_map/ppermute | solution.py:390
  26.5 15.8 %collective-permute-start.5 = (bf16[4,448,128]{2,1,0:T(8,128)(2,1)S(1)}, bf16[4,448,128]{2,1,0:T(8,128)(2,1)S(1)}, u32[]{:S(2)}, u32[]{:S(2)}) collective-permute-start(bf16[4,448,128]{2,1,0:T(8,128)(2,1)S(1)} %pad_maximum_fusion.4), channel_id=1, source_target_pairs={{0,4},{1,5},{2,6},{3,7},{4,0},{5,1},{6,2},{7,3},{8,12},{9,13},{10,... | collective-permute-start | bytes 1376264 | tf_op jit(solution)/shard_map/ppermute | solution.py:390
  28.1 8.0 %collective-permute-start.4 = (bf16[448,128]{1,0:T(8,128)(2,1)S(1)}, bf16[448,128]{1,0:T(8,128)(2,1)S(1)}, u32[]{:S(2)}, u32[]{:S(2)}) collective-permute-start(bf16[448,128]{1,0:T(8,128)(2,1)S(1)} %get-tuple-element.143), channel_id=1, source_target_pairs={{0,16},{1,17},{2,18},{3,19},{4,20},{5,21},{6,22},{7,23},{8,24},{9,... | collective-permute-start | bytes 344072 | tf_op jit(solution)/shard_map/ppermute | solution.py:390
  32.2 10.2 %collective-permute-start.6 = (bf16[4,448,128]{2,1,0:T(8,128)(2,1)S(1)}, bf16[4,448,128]{2,1,0:T(8,128)(2,1)S(1)}, u32[]{:S(2)}, u32[]{:S(2)}) collective-permute-start(bf16[4,448,128]{2,1,0:T(8,128)(2,1)S(1)} %pad_maximum_fusion.5), channel_id=1, source_target_pairs={{0,2},{1,3},{2,0},{3,1},{4,6},{5,7},{6,4},{7,5},{8,10},{9,11},{10,... | collective-permute-start | bytes 1376264 | tf_op jit(solution)/shard_map/ppermute | solution.py:390
  42.5 8.7 %collective-permute-start.8 = (bf16[8,448,128]{2,1,0:T(8,128)(2,1)S(1)}, bf16[8,448,128]{2,1,0:T(8,128)(2,1)S(1)}, u32[]{:S(2)}, u32[]{:S(2)}) collective-permute-start(bf16[8,448,128]{2,1,0:T(8,128)(2,1)S(1)} %pad_maximum_fusion.near.low_near), channel_id=1, source_target_pairs={{0,1},{1,0},{2,3},{3,2},{4,5},{5,4},{6,7},{7,6},{8,9},{9,8},{10,11... | collective-permute-start | bytes 2752520 | tf_op jit(solution)/shard_map/ppermute | solution.py:390
  42.7 8.5 %collective-permute-start.9 = (bf16[8,448,128]{2,1,0:T(8,128)(2,1)S(1)}, bf16[8,448,128]{2,1,0:T(8,128)(2,1)S(1)}, u32[]{:S(2)}, u32[]{:S(2)}) collective-permute-start(bf16[8,448,128]{2,1,0:T(8,128)(2,1)S(1)} %pad_maximum_fusion.1.near), channel_id=1, source_target_pairs={{0,1},{1,0},{2,3},{3,2},{4,5},{5,4},{6,7},{7,6},{8,9},{9,8},{10,11... | collective-permute-start | bytes 2752520 | tf_op jit(solution)/shard_map/ppermute | solution.py:390
  43.3 7.6 %collective-permute-start.10 = (bf16[2,448,128]{2,1,0:T(8,128)(2,1)S(1)}, bf16[2,448,128]{2,1,0:T(8,128)(2,1)S(1)}, u32[]{:S(2)}, u32[]{:S(2)}) collective-permute-start(bf16[2,448,128]{2,1,0:T(8,128)(2,1)S(1)} %get-tuple-element.329), channel_id=1, source_target_pairs={{0,2},{1,3},{2,0},{3,1},{4,6},{5,7},{6,4},{7,5},{8,10},{9,11},{10,... | collective-permute-start | bytes 688136 | tf_op jit(solution)/shard_map/ppermute | solution.py:390
  43.9 7.2 %collective-permute-start.11 = (bf16[2,448,128]{2,1,0:T(8,128)(2,1)S(1)}, bf16[2,448,128]{2,1,0:T(8,128)(2,1)S(1)}, u32[]{:S(2)}, u32[]{:S(2)}) collective-permute-start(bf16[2,448,128]{2,1,0:T(8,128)(2,1)S(1)} %get-tuple-element.328), channel_id=1, source_target_pairs={{0,4},{1,5},{2,6},{3,7},{4,0},{5,1},{6,2},{7,3},{8,12},{9,13},{10,... | collective-permute-start | bytes 688136 | tf_op jit(solution)/shard_map/ppermute | solution.py:390
  51.3 11.4 %collective-permute-start.12 = (bf16[4,448,128]{2,1,0:T(8,128)(2,1)S(1)}, bf16[4,448,128]{2,1,0:T(8,128)(2,1)S(1)}, u32[]{:S(2)}, u32[]{:S(2)}) collective-permute-start(bf16[4,448,128]{2,1,0:T(8,128)(2,1)S(1)} %pad_maximum_fusion.6), channel_id=1, source_target_pairs={{0,4},{1,5},{2,6},{3,7},{4,0},{5,1},{6,2},{7,3},{8,12},{9,13},{10,... | collective-permute-start | bytes 1376264 | tf_op jit(solution)/shard_map/ppermute | solution.py:390
  51.9 11.1 %collective-permute-start.13 = (bf16[4,448,128]{2,1,0:T(8,128)(2,1)S(1)}, bf16[4,448,128]{2,1,0:T(8,128)(2,1)S(1)}, u32[]{:S(2)}, u32[]{:S(2)}) collective-permute-start(bf16[4,448,128]{2,1,0:T(8,128)(2,1)S(1)} %pad_maximum_fusion.7), channel_id=1, source_target_pairs={{0,2},{1,3},{2,0},{3,1},{4,6},{5,7},{6,4},{7,5},{8,10},{9,11},{10,... | collective-permute-start | bytes 1376264 | tf_op jit(solution)/shard_map/ppermute | solution.py:390
  91.1 10.7 %collective-permute-start.17 = (bf16[2,448,128]{2,1,0:T(8,128)(2,1)S(1)}, bf16[2,448,128]{2,1,0:T(8,128)(2,1)S(1)}, u32[]{:S(2)}, u32[]{:S(2)}) collective-permute-start(bf16[2,448,128]{2,1,0:T(8,128)(2,1)S(1)} %get-tuple-element.326), channel_id=1, source_target_pairs={{0,4},{1,5},{2,6},{3,7},{4,0},{5,1},{6,2},{7,3},{8,12},{9,13},{10,... | collective-permute-start | bytes 688136 | tf_op jit(solution)/shard_map/ppermute | solution.py:390
  95.7 7.9 %collective-permute-start.18 = (bf16[2,448,128]{2,1,0:T(8,128)(2,1)S(1)}, bf16[2,448,128]{2,1,0:T(8,128)(2,1)S(1)}, u32[]{:S(2)}, u32[]{:S(2)}) collective-permute-start(bf16[2,448,128]{2,1,0:T(8,128)(2,1)S(1)} %get-tuple-element.324), channel_id=1, source_target_pairs={{0,2},{1,3},{2,0},{3,1},{4,6},{5,7},{6,4},{7,5},{8,10},{9,11},{10,... | collective-permute-start | bytes 688136 | tf_op jit(solution)/shard_map/ppermute | solution.py:390
  101.5 6.9 %collective-permute-start.24 = (bf16[2,4,448,128]{3,2,1,0:T(8,128)(2,1)S(1)}, bf16[2,4,448,128]{3,2,1,0:T(8,128)(2,1)S(1)}, u32[]{:S(2)}, u32[]{:S(2)}) collective-permute-start(bf16[2,4,448,128]{3,2,1,0:T(8,128)(2,1)S(1)} %get-tuple-element.216), channel_id=1, source_target_pairs={{0,1},{1,0},{2,3},{3,2},{4,5},{5,4},{6,7},{7,6},{8,9},{9,8},{10,11... | collective-permute-start | bytes 2752520 | tf_op jit(solution)/shard_map/ppermute | solution.py:390
  103.6 10.8 %collective-permute-start.20 = (bf16[1,448,128]{2,1,0:T(8,128)(2,1)S(1)}, bf16[1,448,128]{2,1,0:T(8,128)(2,1)S(1)}, u32[]{:S(2)}, u32[]{:S(2)}) collective-permute-start(bf16[1,448,128]{2,1,0:T(8,128)(2,1)S(1)} %get-tuple-element.352), channel_id=1, source_target_pairs={{0,2},{1,3},{2,0},{3,1},{4,6},{5,7},{6,4},{7,5},{8,10},{9,11},{10,... | collective-permute-start | bytes 344072 | tf_op jit(solution)/shard_map/ppermute | solution.py:390
  105.2 9.3 %collective-permute-start.21 = (bf16[1,448,128]{2,1,0:T(8,128)(2,1)S(1)}, bf16[1,448,128]{2,1,0:T(8,128)(2,1)S(1)}, u32[]{:S(2)}, u32[]{:S(2)}) collective-permute-start(bf16[1,448,128]{2,1,0:T(8,128)(2,1)S(1)} %get-tuple-element.350), channel_id=1, source_target_pairs={{0,4},{1,5},{2,6},{3,7},{4,0},{5,1},{6,2},{7,3},{8,12},{9,13},{10,... | collective-permute-start | bytes 344072 | tf_op jit(solution)/shard_map/ppermute | solution.py:390
  106.0 8.5 %collective-permute-start.22 = (bf16[2,448,128]{2,1,0:T(8,128)(2,1)S(1)}, bf16[2,448,128]{2,1,0:T(8,128)(2,1)S(1)}, u32[]{:S(2)}, u32[]{:S(2)}) collective-permute-start(bf16[2,448,128]{2,1,0:T(8,128)(2,1)S(1)} %get-tuple-element.322), channel_id=1, source_target_pairs={{0,4},{1,5},{2,6},{3,7},{4,0},{5,1},{6,2},{7,3},{8,12},{9,13},{10,... | collective-permute-start | bytes 688136 | tf_op jit(solution)/shard_map/ppermute | solution.py:390
  119.8 9.5 %collective-permute-start.28 = (bf16[2,448,128]{2,1,0:T(8,128)(2,1)S(1)}, bf16[2,448,128]{2,1,0:T(8,128)(2,1)S(1)}, u32[]{:S(2)}, u32[]{:S(2)}) collective-permute-start(bf16[2,448,128]{2,1,0:T(8,128)(2,1)S(1)} %get-tuple-element.318), channel_id=1, source_target_pairs={{0,4},{1,5},{2,6},{3,7},{4,0},{5,1},{6,2},{7,3},{8,12},{9,13},{10,... | collective-permute-start | bytes 688136 | tf_op jit(solution)/shard_map/ppermute | solution.py:390
  121.5 7.8 %collective-permute-start.29 = (bf16[2,448,128]{2,1,0:T(8,128)(2,1)S(1)}, bf16[2,448,128]{2,1,0:T(8,128)(2,1)S(1)}, u32[]{:S(2)}, u32[]{:S(2)}) collective-permute-start(bf16[2,448,128]{2,1,0:T(8,128)(2,1)S(1)} %get-tuple-element.316), channel_id=1, source_target_pairs={{0,2},{1,3},{2,0},{3,1},{4,6},{5,7},{6,4},{7,5},{8,10},{9,11},{10,... | collective-permute-start | bytes 688136 | tf_op jit(solution)/shard_map/ppermute | solution.py:390
  129.4 9.9 %collective-permute-start.30 = (bf16[2,448,128]{2,1,0:T(8,128)(2,1)S(1)}, bf16[2,448,128]{2,1,0:T(8,128)(2,1)S(1)}, u32[]{:S(2)}, u32[]{:S(2)}) collective-permute-start(bf16[2,448,128]{2,1,0:T(8,128)(2,1)S(1)} %get-tuple-element.314), channel_id=1, source_target_pairs={{0,4},{1,5},{2,6},{3,7},{4,0},{5,1},{6,2},{7,3},{8,12},{9,13},{10,... | collective-permute-start | bytes 688136 | tf_op jit(solution)/shard_map/ppermute | solution.py:390
  130.2 9.2 %collective-permute-start.31 = (bf16[2,448,128]{2,1,0:T(8,128)(2,1)S(1)}, bf16[2,448,128]{2,1,0:T(8,128)(2,1)S(1)}, u32[]{:S(2)}, u32[]{:S(2)}) collective-permute-start(bf16[2,448,128]{2,1,0:T(8,128)(2,1)S(1)} %get-tuple-element.312), channel_id=1, source_target_pairs={{0,2},{1,3},{2,0},{3,1},{4,6},{5,7},{6,4},{7,5},{8,10},{9,11},{10,... | collective-permute-start | bytes 688136 | tf_op jit(solution)/shard_map/ppermute | solution.py:390
  131.1 8.2 %collective-permute-start.32 = (bf16[1,448,128]{2,1,0:T(8,128)(2,1)S(1)}, bf16[1,448,128]{2,1,0:T(8,128)(2,1)S(1)}, u32[]{:S(2)}, u32[]{:S(2)}) collective-permute-start(bf16[1,448,128]{2,1,0:T(8,128)(2,1)S(1)} %get-tuple-element.344), channel_id=1, source_target_pairs={{0,2},{1,3},{2,0},{3,1},{4,6},{5,7},{6,4},{7,5},{8,10},{9,11},{10,... | collective-permute-start | bytes 344072 | tf_op jit(solution)/shard_map/ppermute | solution.py:390
  141.9 7.1 %collective-permute-start.37 = (bf16[448,128]{1,0:T(8,128)(2,1)S(1)}, bf16[448,128]{1,0:T(8,128)(2,1)S(1)}, u32[]{:S(2)}, u32[]{:S(2)}) collective-permute-start(bf16[448,128]{1,0:T(8,128)(2,1)S(1)} %get-tuple-element.336), channel_id=1, source_target_pairs={{0,16},{1,17},{2,18},{3,19},{4,20},{5,21},{6,22},{7,23},{8,24},{9,... | collective-permute-start | bytes 344072 | tf_op jit(solution)/shard_map/ppermute | solution.py:390
  149.1 7.3 %collective-permute-start.38 = (bf16[2,448,128]{2,1,0:T(8,128)(2,1)S(1)}, bf16[2,448,128]{2,1,0:T(8,128)(2,1)S(1)}, u32[]{:S(2)}, u32[]{:S(2)}) collective-permute-start(bf16[2,448,128]{2,1,0:T(8,128)(2,1)S(1)} %pad_maximum_fusion.13), channel_id=1, source_target_pairs={{0,8},{1,9},{2,10},{3,11},{4,12},{5,13},{6,14},{7,15},{8,0},{9,1},... | collective-permute-start | bytes 688136 | tf_op jit(solution)/shard_map/ppermute | solution.py:390
  (22 other events, 128.8 us)
